TPU v7x, 256 devices: a whole 4x4x8 slice. The times are simulated.
256 devices in a mesh: tile: 64 (over x, y, z_lo), frame: 4 (over z_hi, core).
Axes of the slice: x: 4, y: 4, z: 8 (z_hi: 2, z_lo: 4; z = z_hi * 4 + z_lo), core: 2. Of those that a mesh axis runs over, the one named last changes fastest.
Arguments:
- video: float32 [16, 128, 160, 128], P('frame', 'tile'), may hold values from -6 to 6
- norm_gain: float32 [2, 2, 128], replicated, may hold values from 0.1 to 1.9
- space_weight: float32 [2, 3, 3, 128, 128], replicated, may hold values from -0.1875 to 0.1875
- time_weight: float32 [2, 3, 128, 128], replicated, may hold values from -0.3125 to 0.3125
- down_weight: float32 [3, 3, 128, 256], replicated, may hold values from -0.1875 to 0.1875
- attn_gain: float32 [256], replicated, may hold values from 0.1 to 1.9
- w_query: float32 [256, 256], replicated, may hold values from -4 to 4
- w_key: float32 [256, 256], replicated, may hold values from -4 to 4
- w_value: float32 [256, 256], replicated, may hold values from -0.375 to 0.375
- w_out: float32 [256, 256], replicated, may hold values from -0.375 to 0.375
Outputs:
- encoded: float32 [256, 320, 256], P(('frame', 'tile'))
All inputs are finite; a program needn't handle non-finite values.
Results may differ from a plain program's by a relative error of at most 0.0003.
Values sent between devices are 32-bit elements; how exact they have to be, the bound alone decides.
A program may use at most 64 MiB of HBM per device.

v0:
```python
import functools

import jax
import jax.numpy as jnp
from jax import lax
from jax.experimental import pallas as pl
from jax.experimental.pallas import tpu as pltpu
from jax.sharding import PartitionSpec as P

highest = lax.Precision.HIGHEST
MESH = pl.DeviceIdType.MESH
F32 = jnp.float32
BF16 = jnp.bfloat16


def passed_along(shard, axis, by):
    size = lax.axis_size(axis)
    pairs = [(i, i + by) for i in range(size) if 0 <= i + by < size]
    return lax.ppermute(shard, axis, pairs)


def extended(cells, sides, width):
    for axis, dim in sides:
        count = lax.axis_size(axis)
        ends = count - 1
        head = lax.slice_in_dim(cells, 0, width, axis=dim)
        tail = lax.slice_in_dim(cells, cells.shape[dim] - width, cells.shape[dim], axis=dim)
        cells = jnp.concatenate(
            [
                lax.ppermute(tail, axis, [(i, (i + 1) % count) for i in range(ends)]),
                cells,
                lax.ppermute(head, axis, [((i + 1) % count, i) for i in range(ends)]),
            ],
            axis=dim,
        )
    return cells


def norm(values, gain):
    return values * lax.rsqrt(jnp.mean(values * values, -1, keepdims=True) + 1e-06) * gain


def act(values, gain):
    return jax.nn.silu(norm(values, gain))


def conv_rows(inputs, kernel):
    return lax.conv_general_dilated(
        inputs,
        kernel,
        (1, 1),
        ((0, 0), (1, 1)),
        dimension_numbers=("NHWC", "HWIO", "NHWC"),
        precision=highest,
    )


def time_mix(inputs, kernel):
    earlier = passed_along(inputs[-2:], "frame", 1)
    opening = lax.axis_index("frame") == 0
    start = jnp.where(opening, jnp.concatenate([inputs[:1], inputs[:1]], 0), earlier)
    padded = jnp.concatenate([start, inputs], 0)
    count = inputs.shape[0]
    total = jnp.einsum("fhwc,cd->fhwd", padded[0:count], kernel[0], precision=highest)
    total = total + jnp.einsum("fhwc,cd->fhwd", padded[1 : count + 1], kernel[1], precision=highest)
    total = total + jnp.einsum("fhwc,cd->fhwd", padded[2 : count + 2], kernel[2], precision=highest)
    return total


def split(values):
    high = values.astype(BF16)
    return high, (values - high.astype(F32)).astype(BF16)


def three_pass(a, b):
    ah, al = split(a)
    bh, bl = split(b)
    total = jnp.dot(ah, bh, preferred_element_type=F32)
    total = total + jnp.dot(ah, bl, preferred_element_type=F32)
    return total + jnp.dot(al, bh, preferred_element_type=F32)


def dot_f32(a, b, dims=((1,), (0,))):
    return lax.dot_general(a, b, (dims, ((), ())), precision=highest, preferred_element_type=F32)


QT = 128


def attend_kernel(
    z_ref, gain_ref, wq_ref, wk_ref, wv_ref, wo_ref, out_ref,
    keys, query, acc, best, total, normed, part_acc, part_stat, result,
    s1, r1, ss, rs, rets, retr,
):
    tile = lax.axis_index("tile")
    frame = lax.axis_index("frame")
    x, y, z = tile // 16, (tile // 4) % 4, tile % 4
    half, s = z // 2, z % 2
    zh, core = frame // 2, frame % 2

    def dev(x, y, z, core):
        return {"tile": x * 16 + y * 4 + z, "frame": zh * 2 + core}

    up = dev(x, (y + 1) % 4, z, core)
    down = dev(x, (y + 3) % 4, z, core)
    mate = dev(x, y, z + 1 - 2 * s, core)
    sibling = dev(x, y, z, 1 - core)
    sz = 2 * core + s
    crossed = half != core
    idx = y * 4 + sz
    me_q = y * 4 + z

    barrier = pltpu.get_barrier_semaphore()

    def hello(device):
        pl.semaphore_signal(barrier, inc=1, device_id=device, device_id_type=MESH)

    for device in (up, down, mate, sibling):
        hello(device)
    for dx in range(1, 4):
        hello(dev((x + dx) % 4, y, sz, half))

    @pl.when(crossed)
    def _():
        hello(dev(x, y, sz, half))

    for k in range(16):
        sy, ssz, sc = k // 4, 2 * core + (k % 2), (k // 2) % 2

        @pl.when(jnp.logical_not((sy == y) & (ssz == z) & (sc == core)))
        def _():
            hello(dev(x, sy, ssz, sc))

    pl.semaphore_wait(barrier, 22 + 2 * crossed.astype(jnp.int32))

    slot = s * 4 + y
    first = []
    for dx in range(1, 4):
        xt = (x + dx) % 4
        copy = pltpu.make_async_remote_copy(
            src_ref=z_ref.at[xt],
            dst_ref=keys.at[slot, pl.ds(pl.multiple_of(x * 80, 80), 80)],
            send_sem=s1.at[dx],
            recv_sem=r1.at[dx],
            device_id=dev(xt, y, sz, half),
            device_id_type=MESH,
        )
        copy.start()
        first.append(copy)
    cross = pltpu.make_async_remote_copy(
        src_ref=z_ref.at[x],
        dst_ref=keys.at[slot, pl.ds(pl.multiple_of(x * 80, 80), 80)],
        send_sem=s1.at[0],
        recv_sem=r1.at[0],
        device_id=dev(x, y, sz, half),
        device_id_type=MESH,
    )

    @pl.when(crossed)
    def _():
        cross.start()

    @pl.when(jnp.logical_not(crossed))
    def _():
        keys[slot, pl.ds(pl.multiple_of(x * 80, 80), 80), :] = z_ref[x]

    for copy in first:
        copy.wait_recv()

    @pl.when(crossed)
    def _():
        cross.wait_recv()

    slot_up = s * 4 + (y + 1) % 4
    slot_down = s * 4 + (y + 3) % 4
    slot_far = s * 4 + (y + 2) % 4
    other = (1 - s) * 4
    mate_own, mate_up = other + y, other + (y + 1) % 4
    mate_down, mate_far = other + (y + 3) % 4, other + (y + 2) % 4
    lo, hi = pl.ds(0, 160), pl.ds(160, 160)

    def remote(src, dst, device, i):
        return pltpu.make_async_remote_copy(
            src_ref=src, dst_ref=dst, send_sem=ss.at[i], recv_sem=rs.at[i],
            device_id=device, device_id_type=MESH,
        )

    def push(i, block, device, rows=None):
        ref = keys.at[block] if rows is None else keys.at[block, rows]
        copy = remote(ref, ref, device, i)
        copy.start()
        return copy

    def landed(i, block, device, rows=None):
        ref = keys.at[block] if rows is None else keys.at[block, rows]
        remote(ref, ref, device, i).wait_recv()

    sent = [push(0, slot, up), push(1, slot, down), push(2, slot, mate)]

    gain = gain_ref[...]
    own = norm(keys[slot], gain)
    projected = dot_f32(own, wq_ref[...]) * (256.0 ** -0.5)
    query[0] = dot_f32(projected, wk_ref[...], ((1,), (1,)))
    q_copy = remote(query.at[0], query.at[1], sibling, 8)
    q_copy.start()
    sent.append(q_copy)

    best[...] = jnp.full_like(best, -jnp.inf)
    total[...] = jnp.zeros_like(total)
    acc[...] = jnp.zeros_like(acc)

    def attend(block, which):
        normed[...] = norm(keys[block], gain)

        def tile_step(t, _):
            rows = pl.ds(pl.multiple_of(t * 64, 64), 64)
            k = normed[...]
            scores = dot_f32(query[which, rows, :], k, ((1,), (1,)))
            old = best[which, rows, :]
            new = jnp.maximum(old, jnp.max(scores, axis=1, keepdims=True))
            factor = jnp.exp(old - new)
            weights = jnp.exp(scores - new)
            total[which, rows, :] = total[which, rows, :] * factor + jnp.sum(weights, axis=1, keepdims=True)
            best[which, rows, :] = new
            acc[which, rows, :] = acc[which, rows, :] * factor + three_pass(weights, k)
            return 0

        lax.fori_loop(0, 5, tile_step, 0)

    def attend_both(block):
        attend(block, 1)
        attend(block, 0)

    attend(slot, 0)
    q_copy.wait_recv()
    attend(slot, 1)
    landed(0, slot_down, up)
    sent.append(push(5, slot_down, up, lo))
    landed(1, slot_up, down)
    sent.append(push(6, slot_up, down, hi))
    landed(2, mate_own, mate)
    sent.append(push(3, mate_own, up))
    sent.append(push(4, mate_own, down))
    attend_both(slot_down)
    attend_both(slot_up)
    landed(5, slot_far, up, lo)
    landed(6, slot_far, down, hi)
    sent.append(push(7, slot_far, mate))
    attend_both(mate_own)
    attend_both(slot_far)
    landed(3, mate_down, up)
    attend_both(mate_down)
    landed(4, mate_up, down)
    attend_both(mate_up)
    landed(7, mate_far, mate)
    attend(mate_far, 1)
    part_stat[0, 0, :, :] = jnp.broadcast_to(best[1], (320, 128))
    part_stat[0, 1, :, :] = jnp.broadcast_to(total[1], (320, 128))
    merge = [
        remote(acc.at[1], part_acc, sibling, 9),
        remote(part_stat.at[0], part_stat.at[1], sibling, 10),
    ]
    for copy in merge:
        copy.start()
    attend(mate_far, 0)
    for copy in merge:
        copy.wait_recv()
    sent.extend(merge)
    other_best = part_stat[1, 0, :, 0:1]
    other_total = part_stat[1, 1, :, 0:1]
    top = jnp.maximum(best[0], other_best)
    mine_f = jnp.exp(best[0] - top)
    other_f = jnp.exp(other_best - top)
    whole = total[0] * mine_f + other_total * other_f
    mixed = (acc[0] * mine_f + part_acc[...] * other_f) / whole
    value = dot_f32(mixed, wv_ref[...])
    y_out = keys[slot] + dot_f32(value, wo_ref[...])
    for q in range(16):
        for b in range(4):
            start = b * 80 + q * 5
            result[q, b] = y_out[start : start + 5]

    backs = []
    for k in range(16):
        q = (me_q + k) % 16
        copy = pltpu.make_async_remote_copy(
            src_ref=result.at[q],
            dst_ref=out_ref.at[:, idx],
            send_sem=rets.at[k],
            recv_sem=retr.at[idx],
            device_id=dev(x, q // 4, q % 4, half),
            device_id_type=MESH,
        )
        backs.append(copy)
        if k > 0:
            copy.start()

    @pl.when(crossed)
    def _():
        backs[0].start()

    @pl.when(jnp.logical_not(crossed))
    def _():
        out_ref[:, pl.ds(idx, 1), :, :] = result[me_q][:, None]

    for copy in first:
        copy.wait_send()

    @pl.when(crossed)
    def _():
        cross.wait_send()
        backs[0].wait_send()

    for copy in sent:
        copy.wait_send()
    for k in range(16):
        if k > 0:
            backs[k].wait_send()
        sy, ssz, sc = k // 4, 2 * core + (k % 2), (k // 2) % 2

        @pl.when(jnp.logical_not((sy == y) & (ssz == z) & (sc == core)))
        def _():
            pltpu.make_async_remote_copy(
                src_ref=result.at[0],
                dst_ref=out_ref.at[:, k],
                send_sem=rets.at[k],
                recv_sem=retr.at[k],
                device_id=sibling,
                device_id_type=MESH,
            ).wait_recv()


def attend_all(lowered, attn_gain, w_query, w_key, w_value, w_out):
    vmem = pl.BlockSpec(memory_space=pltpu.VMEM)
    dma = pltpu.SemaphoreType.DMA
    out = pl.pallas_call(
        attend_kernel,
        out_shape=jax.ShapeDtypeStruct((4, 16, 5, 256), F32),
        in_specs=[vmem] * 6,
        out_specs=vmem,
        scratch_shapes=[
            pltpu.VMEM((8, 320, 256), F32),
            pltpu.VMEM((2, 320, 256), F32),
            pltpu.VMEM((2, 320, 256), F32),
            pltpu.VMEM((2, 320, 1), F32),
            pltpu.VMEM((2, 320, 1), F32),
            pltpu.VMEM((320, 256), F32),
            pltpu.VMEM((320, 256), F32),
            pltpu.VMEM((2, 2, 320, 128), F32),
            pltpu.VMEM((16, 4, 5, 256), F32),
            dma((4,)), dma((4,)), dma((11,)), dma((11,)), dma((16,)), dma((16,)),
        ],
        compiler_params=pltpu.CompilerParams(
            collective_id=1, has_side_effects=True, vmem_limit_bytes=40 * 2**20
        ),
        name="attend",
    )(lowered, attn_gain.reshape(1, 256), w_query, w_key, w_value, w_out)
    return out.reshape(1, 320, 256)


def local(
    video,
    norm_gain,
    space_weight,
    time_weight,
    down_weight,
    attn_gain,
    w_query,
    w_key,
    w_value,
    w_out,
):
    state = video
    for block in range(2):
        wide = extended(act(state, norm_gain[block, 0]), (("tile", 1),), 1)
        mixed = conv_rows(wide, space_weight[block])
        state = state + time_mix(act(mixed, norm_gain[block, 1]), time_weight[block])
    upper = passed_along(state[:, -1:], "tile", 1)
    stacked = jnp.concatenate([upper, state], 1)
    lowered = lax.conv_general_dilated(
        stacked,
        down_weight,
        (2, 2),
        ((0, 0), (1, 0)),
        dimension_numbers=("NHWC", "HWIO", "NHWC"),
        precision=highest,
    )
    lowered = lowered.reshape(4, 80, 256)
    return attend_all(lowered, attn_gain, w_query, w_key, w_value, w_out)


def solution(mesh):
    in_specs = (P("frame", "tile", None, None), P(), P(), P(), P(), P(), P(), P(), P(), P())
    out_specs = P(("frame", "tile"), None, None)
    return jax.shard_map(local, mesh=mesh, in_specs=in_specs, out_specs=out_specs, check_vma=False)
```

profile of v0, /device:TPU:232, one launch (start us, length us, event | category | flops | bytes accessed | tf_op | source)
XLA Modules:
  0.0 210.3 jit_solution(14129298818351113868)
XLA Ops:
  0.0 0.8 slice_bitcast_fusion
  0.8 1.4 multiply_reduce_fusion.3
  2.3 1.3 divide_multiply_fusion.3
  3.7 4.8 %collective-permute-start = (f32[4,1,160,128]{3,2,1,0:T(8,128)S(1)}, f32[4,1,160,128]{3,2,1,0:T(8,128)S(1)}, u32[]{:S(2)}, u32[]{:S(2)}) collective-permute-start(f32[4,1,160,128]{3,2,1,0:T(8,128)S(1)} %get-tuple-element.7), channel_id=1, source_target_pairs={{0,4},{4,8},{8,12},{12,16},{16,20},{20,24},{24,28},{28,32},{32,36}... | collective-permute-start | bytes 983048 | tf_op jit(solution)/shard_map/ppermute | solution.py:30
  8.5 0.0 copy-start.7
  8.5 2.1 collective-permute-start.1
  10.6 6.1 %collective-permute-done = f32[4,1,160,128]{3,2,1,0:T(8,128)S(1)} collective-permute-done((f32[4,1,160,128]{3,2,1,0:T(8,128)S(1)}, f32[4,1,160,128]{3,2,1,0:T(8,128)S(1)}, u32[]{:S(2)}, u32[]{:S(2)}) %collective-permute-start) | collective-permute-done | bytes 327712 | tf_op jit(solution)/shard_map/ppermute | solution.py:30
  16.7 7.3 %collective-permute-done.1 = f32[4,1,160,128]{3,2,1,0:T(8,128)S(1)} collective-permute-done((f32[4,1,160,128]{3,2,1,0:T(8,128)S(1)}, f32[4,1,160,128]{3,2,1,0:T(8,128)S(1)}, u32[]{:S(2)}, u32[]{:S(2)}) %collective-permute-start.1) | collective-permute-done | bytes 327712 | tf_op jit(solution)/shard_map/ppermute | solution.py:32
  24.0 0.1 pad_maximum_fusion
  24.1 0.0 copy-done.7
  24.1 7.4 %multiply_reduce_fusion.2 = (f32[4,2,160]{0,2,1:T(8,128)S(1)}, f32[4,2,160,128]{3,0,2,1:T(4,128)S(1)}) fusion(f32[2,3,3,128,128]{4,3,2,1,0:T(8,128)S(1)} %copy-done.7, f32[4,4,160,128]{3,2,1,0:T(8,128)S(1)} %pad_maximum_fusion), kind=kOutput, calls=%fused_computation.28 | convolution fusion | flops 2255813376 | bytes 2561024 | tf_op jit(solution)/shard_map/conv_general_dilated | solution.py:48
  31.6 0.0 copy-start.9
  31.6 0.1 copy.86
  31.7 0.3 divide_multiply_fusion.2
  32.0 1.9 collective-permute-start.2
  34.0 0.7 fusion.22
  34.6 0.0 copy-start.6
  34.7 10.8 %collective-permute-done.2 = f32[2,2,160,128]{3,2,1,0:T(8,128)S(1)} collective-permute-done((f32[2,2,160,128]{3,2,1,0:T(8,128)S(1)}, f32[2,2,160,128]{3,2,1,0:T(8,128)S(1)}, u32[]{:S(2)}, u32[]{:S(2)}) %collective-permute-start.2) | collective-permute-done | bytes 327712 | tf_op jit(solution)/shard_map/ppermute | solution.py:19
  45.5 0.7 fusion.11
  46.2 0.0 copy-done.6
  46.2 0.9 multiply_reduce_fusion.1
  47.1 0.3 divide_multiply_fusion.1
  47.4 7.7 %collective-permute-start.3 = (f32[4,1,160,128]{3,2,1,0:T(8,128)S(1)}, f32[4,1,160,128]{3,2,1,0:T(8,128)S(1)}, u32[]{:S(2)}, u32[]{:S(2)}) collective-permute-start(f32[4,1,160,128]{3,2,1,0:T(8,128)S(1)} %get-tuple-element.5), channel_id=1, source_target_pairs={{0,4},{4,8},{8,12},{12,16},{16,20},{20,24},{24,28},{28,32},{32,36}... | collective-permute-start | bytes 983048 | tf_op jit(solution)/shard_map/ppermute | solution.py:30
  55.1 0.0 copy-start.8
  55.2 6.8 %collective-permute-start.4 = (f32[4,1,160,128]{3,2,1,0:T(8,128)S(1)}, f32[4,1,160,128]{3,2,1,0:T(8,128)S(1)}, u32[]{:S(2)}, u32[]{:S(2)}) collective-permute-start(f32[4,1,160,128]{3,2,1,0:T(8,128)S(1)} %get-tuple-element.6), channel_id=1, source_target_pairs={{4,0},{8,4},{12,8},{16,12},{20,16},{24,20},{28,24},{32,28},{36,32}... | collective-permute-start | bytes 983048 | tf_op jit(solution)/shard_map/ppermute | solution.py:32
  61.9 2.8 %collective-permute-done.3 = f32[4,1,160,128]{3,2,1,0:T(8,128)S(1)} collective-permute-done((f32[4,1,160,128]{3,2,1,0:T(8,128)S(1)}, f32[4,1,160,128]{3,2,1,0:T(8,128)S(1)}, u32[]{:S(2)}, u32[]{:S(2)}) %collective-permute-start.3) | collective-permute-done | bytes 327712 | tf_op jit(solution)/shard_map/ppermute | solution.py:30
  64.7 6.0 %collective-permute-done.4 = f32[4,1,160,128]{3,2,1,0:T(8,128)S(1)} collective-permute-done((f32[4,1,160,128]{3,2,1,0:T(8,128)S(1)}, f32[4,1,160,128]{3,2,1,0:T(8,128)S(1)}, u32[]{:S(2)}, u32[]{:S(2)}) %collective-permute-start.4) | collective-permute-done | bytes 327712 | tf_op jit(solution)/shard_map/ppermute | solution.py:32
  70.7 0.1 pad_maximum_fusion.1
  70.8 7.4 %multiply_reduce_fusion = (f32[4,2,160]{0,2,1:T(8,128)S(1)}, f32[4,2,160,128]{3,0,2,1:T(4,128)S(1)}) fusion(f32[2,3,3,128,128]{4,3,2,1,0:T(8,128)S(1)} %copy-done.8, f32[4,4,160,128]{3,2,1,0:T(8,128)S(1)} %pad_maximum_fusion.1), kind=kOutput, calls=%fused_computation.24 | convolution fusion | flops 2255813376 | bytes 2561024 | tf_op jit(solution)/shard_map/conv_general_dilated | solution.py:48
  78.3 0.1 copy.93
  78.4 0.3 divide_multiply_fusion
  78.7 1.9 collective-permute-start.5
  80.7 0.7 fusion.18
  81.3 11.3 %collective-permute-done.5 = f32[2,2,160,128]{3,2,1,0:T(8,128)S(1)} collective-permute-done((f32[2,2,160,128]{3,2,1,0:T(8,128)S(1)}, f32[2,2,160,128]{3,2,1,0:T(8,128)S(1)}, u32[]{:S(2)}, u32[]{:S(2)}) %collective-permute-start.5) | collective-permute-done | bytes 327712 | tf_op jit(solution)/shard_map/ppermute | solution.py:19
  92.7 0.7 fusion.10
  93.3 0.7 fusion.7
  94.1 3.1 %collective-permute-start.6 = (f32[4,1,160,128]{3,2,1,0:T(8,128)S(1)}, f32[4,1,160,128]{3,2,1,0:T(8,128)S(1)}, u32[]{:S(2)}, u32[]{:S(2)}) collective-permute-start(f32[4,1,160,128]{3,2,1,0:T(8,128)S(1)} %slice.124), channel_id=1, source_target_pairs={{0,4},{4,8},{8,12},{12,16},{16,20},{20,24},{24,28},{28,32},{32,36}... | collective-permute-start | bytes 983048 | tf_op jit(solution)/shard_map/ppermute | solution.py:19
  97.2 5.8 %collective-permute-done.6 = f32[4,1,160,128]{3,2,1,0:T(8,128)S(1)} collective-permute-done((f32[4,1,160,128]{3,2,1,0:T(8,128)S(1)}, f32[4,1,160,128]{3,2,1,0:T(8,128)S(1)}, u32[]{:S(2)}, u32[]{:S(2)}) %collective-permute-start.6) | collective-permute-done | bytes 327712 | tf_op jit(solution)/shard_map/ppermute | solution.py:19
  103.0 0.1 pad_maximum_fusion.4
  103.1 0.0 copy-start.1
  103.1 0.0 copy-start.2
  103.1 0.0 copy-start.3
  103.1 0.0 copy-start.4
  103.2 0.0 copy-start.5
  103.2 3.2 %fusion.8 = f32[4,1,80,256]{3,0,2,1:T(4,128)S(1)} fusion(f32[3,3,128,256]{3,2,1,0:T(8,128)S(1)} %copy-done, f32[4,3,160,128]{3,2,1,0:T(8,128)S(1)} %pad_maximum_fusion.4), kind=kOutput, calls=%fused_computation.15 | convolution fusion | flops 1127743488 | bytes 2490368 | tf_op jit(solution)/shard_map/conv_general_dilated | solution.py:380
  106.4 0.1 copy.140
  106.5 102.9 %attend.1 = f32[4,16,5,256]{3,2,1,0:T(8,128)S(1)} custom-call(f32[4,80,256]{2,1,0:T(8,128)S(1)} %bitcast.69, f32[1,256]{1,0:T(1,128)S(1)} %bitcast.70, f32[256,256]{1,0:T(8,128)S(1)} %copy-done.1, f32[256,256]{1,0:T(8,128)S(1)} %copy-done.2, f32[256,256]{1,0:T(8,128)S(1)} %copy-done.3, f32[256,256]{1,0:T(8,128)S(1)} %copy-done.4), custom_call_target="tpu_custom_call" | custom-call | tf_op jit(solution)/shard_map/attend/pallas_call | solution.py:336
  209.5 0.8 reshape.59
  (24 shorter events, 0.4 us)
Async XLA Ops:
  0.0 103.1 %copy-start = (f32[3,3,128,256]{3,2,1,0:T(8,128)S(1)}, f32[3,3,128,256]{3,2,1,0:T(8,128)}, u32[]{:S(2)}) copy-start(f32[3,3,128,256]{3,2,1,0:T(8,128)} %param.14) | copy-start | bytes 3538948
  3.7 13.0 %collective-permute-start = (f32[4,1,160,128]{3,2,1,0:T(8,128)S(1)}, f32[4,1,160,128]{3,2,1,0:T(8,128)S(1)}, u32[]{:S(2)}, u32[]{:S(2)}) collective-permute-start(f32[4,1,160,128]{3,2,1,0:T(8,128)S(1)} %get-tuple-element.7), channel_id=1, source_target_pairs={{0,4},{4,8},{8,12},{12,16},{16,20},{20,24},{24,28},{28,32},{32,36}... | collective-permute-start | bytes 983048 | tf_op jit(solution)/shard_map/ppermute | solution.py:30
  8.5 15.6 %copy-start.7 = (f32[2,3,3,128,128]{4,3,2,1,0:T(8,128)S(1)}, f32[2,3,3,128,128]{4,3,2,1,0:T(8,128)}, u32[]{:S(2)}) copy-start(f32[2,3,3,128,128]{4,3,2,1,0:T(8,128)} %param.12) | copy-start | bytes 3538948
  8.5 15.4 %collective-permute-start.1 = (f32[4,1,160,128]{3,2,1,0:T(8,128)S(1)}, f32[4,1,160,128]{3,2,1,0:T(8,128)S(1)}, u32[]{:S(2)}, u32[]{:S(2)}) collective-permute-start(f32[4,1,160,128]{3,2,1,0:T(8,128)S(1)} %get-tuple-element.8), channel_id=1, source_target_pairs={{4,0},{8,4},{12,8},{16,12},{20,16},{24,20},{28,24},{32,28},{36,32}... | collective-permute-start | bytes 983048 | tf_op jit(solution)/shard_map/ppermute | solution.py:32
  31.6 2.4 %copy-start.9 = (f32[2,3,128,128]{3,2,1,0:T(8,128)S(1)}, f32[2,3,128,128]{3,2,1,0:T(8,128)}, u32[]{:S(2)}) copy-start(f32[2,3,128,128]{3,2,1,0:T(8,128)} %param.13) | copy-start | bytes 1179652
  32.0 13.5 %collective-permute-start.2 = (f32[2,2,160,128]{3,2,1,0:T(8,128)S(1)}, f32[2,2,160,128]{3,2,1,0:T(8,128)S(1)}, u32[]{:S(2)}, u32[]{:S(2)}) collective-permute-start(f32[2,2,160,128]{3,2,1,0:T(8,128)S(1)} %slice.119), channel_id=1, source_target_pairs={{0,1},{1,2},{2,3},{4,5},{5,6},{6,7},{8,9},{9,10},{10,11},{12,13},{... | collective-permute-start | bytes 983048 | tf_op jit(solution)/shard_map/ppermute | solution.py:19
  34.6 11.6 %copy-start.6 = (f32[4,2,160,128]{3,2,1,0:T(8,128)S(1)}, f32[4,2,160,128]{3,2,1,0:T(8,128)}, u32[]{:S(2)}) copy-start(f32[4,2,160,128]{3,2,1,0:T(8,128)} %param.10) | copy-start | bytes 1966084
  47.4 17.3 %collective-permute-start.3 = (f32[4,1,160,128]{3,2,1,0:T(8,128)S(1)}, f32[4,1,160,128]{3,2,1,0:T(8,128)S(1)}, u32[]{:S(2)}, u32[]{:S(2)}) collective-permute-start(f32[4,1,160,128]{3,2,1,0:T(8,128)S(1)} %get-tuple-element.5), channel_id=1, source_target_pairs={{0,4},{4,8},{8,12},{12,16},{16,20},{20,24},{24,28},{28,32},{32,36}... | collective-permute-start | bytes 983048 | tf_op jit(solution)/shard_map/ppermute | solution.py:30
  55.1 15.7 %copy-start.8 = (f32[2,3,3,128,128]{4,3,2,1,0:T(8,128)S(1)}, f32[2,3,3,128,128]{4,3,2,1,0:T(8,128)}, u32[]{:S(2)}) copy-start(f32[2,3,3,128,128]{4,3,2,1,0:T(8,128)} %param.12) | copy-start | bytes 3538948
  55.2 15.6 %collective-permute-start.4 = (f32[4,1,160,128]{3,2,1,0:T(8,128)S(1)}, f32[4,1,160,128]{3,2,1,0:T(8,128)S(1)}, u32[]{:S(2)}, u32[]{:S(2)}) collective-permute-start(f32[4,1,160,128]{3,2,1,0:T(8,128)S(1)} %get-tuple-element.6), channel_id=1, source_target_pairs={{4,0},{8,4},{12,8},{16,12},{20,16},{24,20},{28,24},{32,28},{36,32}... | collective-permute-start | bytes 983048 | tf_op jit(solution)/shard_map/ppermute | solution.py:32
  78.7 13.9 %collective-permute-start.5 = (f32[2,2,160,128]{3,2,1,0:T(8,128)S(1)}, f32[2,2,160,128]{3,2,1,0:T(8,128)S(1)}, u32[]{:S(2)}, u32[]{:S(2)}) collective-permute-start(f32[2,2,160,128]{3,2,1,0:T(8,128)S(1)} %slice.123), channel_id=1, source_target_pairs={{0,1},{1,2},{2,3},{4,5},{5,6},{6,7},{8,9},{9,10},{10,11},{12,13},{... | collective-permute-start | bytes 983048 | tf_op jit(solution)/shard_map/ppermute | solution.py:19
  94.1 9.0 %collective-permute-start.6 = (f32[4,1,160,128]{3,2,1,0:T(8,128)S(1)}, f32[4,1,160,128]{3,2,1,0:T(8,128)S(1)}, u32[]{:S(2)}, u32[]{:S(2)}) collective-permute-start(f32[4,1,160,128]{3,2,1,0:T(8,128)S(1)} %slice.124), channel_id=1, source_target_pairs={{0,4},{4,8},{8,12},{12,16},{16,20},{20,24},{24,28},{28,32},{32,36}... | collective-permute-start | bytes 983048 | tf_op jit(solution)/shard_map/ppermute | solution.py:19
  103.1 3.4 %copy-start.1 = (f32[256,256]{1,0:T(8,128)S(1)}, f32[256,256]{1,0:T(8,128)}, u32[]{:S(2)}) copy-start(f32[256,256]{1,0:T(8,128)} %wq_ref.1) | copy-start | bytes 786436
  103.1 3.4 %copy-start.2 = (f32[256,256]{1,0:T(8,128)S(1)}, f32[256,256]{1,0:T(8,128)}, u32[]{:S(2)}) copy-start(f32[256,256]{1,0:T(8,128)} %wk_ref.1) | copy-start | bytes 786436
  103.1 3.4 %copy-start.3 = (f32[256,256]{1,0:T(8,128)S(1)}, f32[256,256]{1,0:T(8,128)}, u32[]{:S(2)}) copy-start(f32[256,256]{1,0:T(8,128)} %wv_ref.1) | copy-start | bytes 786436
  103.1 3.4 %copy-start.4 = (f32[256,256]{1,0:T(8,128)S(1)}, f32[256,256]{1,0:T(8,128)}, u32[]{:S(2)}) copy-start(f32[256,256]{1,0:T(8,128)} %wo_ref.1) | copy-start | bytes 786436
  103.2 3.4 %copy-start.5 = (f32[256]{0:T(256)S(1)}, f32[256]{0:T(256)}, u32[]{:S(2)}) copy-start(f32[256]{0:T(256)} %param.15) | copy-start | bytes 3076
where the time goes:
time: 211 us; the launch traced here: 210 us
  Pallas kernels  103 us (49%)
  waiting for transfers between devices  50.1 us (24%)
  starting transfers between devices  28.3 us (13%)
  matrix products  22.3 us (11%)
  other arithmetic  3.97 us (2%)
  local copies, waits for them, and re-layouts  2.15 us (1%)
    pallas_call x1, Pallas kernels, attend_all(): pl.pallas_call(attend_kernel, out_shape=jax.ShapeDtypeStruct((4, 16, 5, 2...  103 us
    ppermute x3, waiting for transfers between devices, passed_along(): return lax.ppermute(shard, axis, pairs)  28 us
    conv_general_dilated x2, matrix products, conv_rows(): lax.conv_general_dilated(inputs, kernel, (1, 1), ((0, 0), (1, 1)), dimens...  14.9 us
    ppermute x2, waiting for transfers between devices, extended(): lax.ppermute(head, axis, [((i + 1) % count, i) for i in range(ends)])  13.3 us
    ppermute x2, starting transfers between devices, extended(): lax.ppermute(tail, axis, [(i, (i + 1) % count) for i in range(ends)])  12.5 us
    ppermute x2, waiting for transfers between devices, extended(): lax.ppermute(tail, axis, [(i, (i + 1) % count) for i in range(ends)])  8.85 us
    ppermute x2, starting transfers between devices, extended(): lax.ppermute(head, axis, [((i + 1) % count, i) for i in range(ends)])  8.81 us
    ppermute x3, starting transfers between devices, passed_along(): return lax.ppermute(shard, axis, pairs)  6.97 us
  transfers between devices with their start and end apart: 7, of which 7 were waited for; matrix products, arithmetic and copies ran while one was open for 1% of the time, Pallas kernels for 0%

commit v1 on v0

--- a/solution.py
+++ b/solution.py
@@ -13,63 +13,359 @@
 BF16 = jnp.bfloat16
 
 
-def passed_along(shard, axis, by):
-    size = lax.axis_size(axis)
-    pairs = [(i, i + by) for i in range(size) if 0 <= i + by < size]
-    return lax.ppermute(shard, axis, pairs)
-
-
-def extended(cells, sides, width):
-    for axis, dim in sides:
-        count = lax.axis_size(axis)
-        ends = count - 1
-        head = lax.slice_in_dim(cells, 0, width, axis=dim)
-        tail = lax.slice_in_dim(cells, cells.shape[dim] - width, cells.shape[dim], axis=dim)
-        cells = jnp.concatenate(
-            [
-                lax.ppermute(tail, axis, [(i, (i + 1) % count) for i in range(ends)]),
-                cells,
-                lax.ppermute(head, axis, [((i + 1) % count, i) for i in range(ends)]),
-            ],
-            axis=dim,
-        )
-    return cells
-
-
 def norm(values, gain):
     return values * lax.rsqrt(jnp.mean(values * values, -1, keepdims=True) + 1e-06) * gain
-
-
-def act(values, gain):
-    return jax.nn.silu(norm(values, gain))
-
-
-def conv_rows(inputs, kernel):
-    return lax.conv_general_dilated(
-        inputs,
-        kernel,
-        (1, 1),
-        ((0, 0), (1, 1)),
-        dimension_numbers=("NHWC", "HWIO", "NHWC"),
-        precision=highest,
-    )
-
-
-def time_mix(inputs, kernel):
-    earlier = passed_along(inputs[-2:], "frame", 1)
-    opening = lax.axis_index("frame") == 0
-    start = jnp.where(opening, jnp.concatenate([inputs[:1], inputs[:1]], 0), earlier)
-    padded = jnp.concatenate([start, inputs], 0)
-    count = inputs.shape[0]
-    total = jnp.einsum("fhwc,cd->fhwd", padded[0:count], kernel[0], precision=highest)
-    total = total + jnp.einsum("fhwc,cd->fhwd", padded[1 : count + 1], kernel[1], precision=highest)
-    total = total + jnp.einsum("fhwc,cd->fhwd", padded[2 : count + 2], kernel[2], precision=highest)
-    return total
 
 
 def split(values):
     high = values.astype(BF16)
     return high, (values - high.astype(F32)).astype(BF16)
+
+
+LEFT, RIGHT = 7, 48
+
+
+def act(values, gain):
+    scaled = values * lax.rsqrt(jnp.mean(values * values, -1, keepdims=True) + 1e-06) * gain
+    return scaled / (1.0 + jnp.exp(-scaled))
+
+
+def conv_kernel(
+    video_ref, gain_ref, space_ref, time_ref, down_ref, out_ref,
+    state, padded, ext, ext_in, cols, cols_in, corners, corners_in,
+    late, late_in, u_hi, u_lo, a_hi, a_lo, d_hi, d_lo, w_space, w_time, w_hi, w_lo,
+    send_sems, recv_sems,
+):
+    tile = lax.axis_index("tile")
+    frame = lax.axis_index("frame")
+    k, z = tile // 4, tile % 4
+    has_up, has_down = k > 0, k < 15
+    has_left, has_right = z > 0, z < 3
+
+    def dev(k, z, frame=frame):
+        return {"tile": k * 4 + z, "frame": frame}
+
+    def when(cond, fn):
+        if cond is None:
+            fn()
+        else:
+            pl.when(cond)(fn)
+
+    ids = {}
+    sent = []
+
+    def message(name, src, dst, device):
+        i = ids.setdefault(name, len(ids))
+        return pltpu.make_async_remote_copy(
+            src_ref=src, dst_ref=dst, send_sem=send_sems.at[i], recv_sem=recv_sems.at[i],
+            device_id=device, device_id_type=MESH,
+        )
+
+    def start(name, src, dst, device, cond=None):
+        copy = message(name, src, dst, device)
+        when(cond, copy.start)
+        sent.append((copy, cond))
+
+    def arrived(name, ref, cond=None):
+        copy = message(name, ref, ref, dev(k, (z + 1) % 4))
+        when(cond, copy.wait_recv)
+
+    for b in range(3):
+        padded[b, :, :, 0:8, :] = jnp.zeros((4, 10, 8, 128), F32)
+        padded[b, :, :, 48:56, :] = jnp.zeros((4, 10, 8, 128), F32)
+
+        @pl.when(jnp.logical_not(has_up))
+        def _():
+            padded[b, :, 0, :, :] = jnp.zeros((4, 56, 128), F32)
+
+        @pl.when(jnp.logical_not(has_down))
+        def _():
+            padded[b, :, 9, :, :] = jnp.zeros((4, 56, 128), F32)
+
+    barrier = pltpu.get_barrier_semaphore()
+
+    def hello(device, cond=None):
+        when(cond, lambda: pl.semaphore_signal(barrier, inc=1, device_id=device, device_id_type=MESH))
+
+    sides = ((-1, has_up), (1, has_down))
+    flanks = ((-1, has_left), (1, has_right))
+    for dz in range(1, 4):
+        hello(dev(k, (z + dz) % 4))
+    for dk, ok in sides:
+        hello(dev((k + dk) % 16, z), ok)
+        for dz, fine in flanks:
+            hello(dev((k + dk) % 16, (z + dz) % 4), ok & fine)
+    hello(dev(k, z, (frame + 3) % 4), frame > 0)
+    count = 3 + (frame < 3).astype(jnp.int32)
+    across = 1 + has_left.astype(jnp.int32) + has_right.astype(jnp.int32)
+    count = count + (has_up.astype(jnp.int32) + has_down.astype(jnp.int32)) * across
+    pl.semaphore_wait(barrier, count)
+
+    order = (2, 3, 0, 1)
+    for part in range(4):
+        for fr in range(4):
+            if part == 0:
+                ext[part, fr, 0:2] = jnp.zeros((2, 1, 128), F32)
+            else:
+                ext[part, fr, 0:2] = video_ref[fr, :, 40 * part - 1 : 40 * part, :]
+            if part == 3:
+                ext[part, fr, 2:4] = jnp.zeros((2, 1, 128), F32)
+            else:
+                ext[part, fr, 2:4] = video_ref[fr, :, 40 * part + 40 : 40 * part + 41, :]
+
+    def band(part):
+        return pl.ds(pl.multiple_of(part * 40, 8), 40)
+
+    for dz in (2, 1, 3):
+        part = (z + dz) % 4
+        start(("ext", dz), ext.at[part], ext_in.at[z], dev(k, part))
+    for fr in order:
+        for dz in (2, 1, 3):
+            part = (z + dz) % 4
+            start(("band", fr, dz), video_ref.at[fr, :, band(part), :], state.at[fr, pl.ds(z * 2, 2)], dev(k, part))
+    ext_in[z] = ext[z]
+    for fr in range(4):
+        state[fr, pl.ds(z * 2, 2)] = video_ref[fr, :, band(z), :]
+
+    for b in range(2):
+        for tap in range(9):
+            rows = slice(tap * 128, tap * 128 + 128)
+            high, low = split(space_ref[b, rows, :])
+            w_space[b, rows, 0:128] = high
+            w_space[b, rows, 128:256] = low
+        high, low = split(time_ref[b])
+        w_time[b, :, 0:128] = high
+        w_time[b, :, 128:256] = low
+    for tap in range(9):
+        rows = slice(tap * 128, tap * 128 + 128)
+        high, low = split(down_ref[rows, :])
+        w_hi[rows, :] = high
+        w_lo[rows, :] = low
+
+    def two_part(high, low, weight):
+        both = jnp.dot(high, weight, preferred_element_type=F32)
+        rest = jnp.dot(low, weight[:, 0:128], preferred_element_type=F32)
+        return both[:, 0:128] + both[:, 128:256] + rest
+
+    inner = pl.ds(8, 40)
+
+    def send_rows(b, f0, nf, width, both=True):
+        f = pl.ds(f0, nf)
+        start(("row", b, f0, 1), padded.at[b, f, 8, width, :], padded.at[b, f, 0, width, :], dev((k + 1) % 16, z), has_down)
+        if both:
+            start(("row", b, f0, -1), padded.at[b, f, 1, width, :], padded.at[b, f, 9, width, :], dev((k + 15) % 16, z), has_up)
+
+    def rows_arrived(b, f0, nf, width, both=True):
+        f = pl.ds(f0, nf)
+        arrived(("row", b, f0, 1), padded.at[b, f, 0, width, :], has_up)
+        if both:
+            arrived(("row", b, f0, -1), padded.at[b, f, 9, width, :], has_down)
+
+    def directions(both):
+        return ((1, 1), (1, -1), (-1, 1), (-1, -1)) if both else ((1, 1),)
+
+    def send_edges(b, f0, nf, both=True):
+        f = pl.ds(f0, nf)
+        for fr in range(f0, f0 + nf):
+            cols[b - 1, 1, fr] = padded[b, fr, 1:9, 47:48, :]
+            if both:
+                cols[b - 1, 0, fr] = padded[b, fr, 1:9, 8:9, :]
+            for dk, dz in directions(both):
+                row, col = 8 if dk > 0 else 1, 47 if dz > 0 else 8
+                corners[b - 1, (dk > 0) * 2 + (dz > 0), fr] = padded[b, fr, row, col : col + 1, :]
+        start(("col", b, f0, 1), cols.at[b - 1, 1, f], cols_in.at[b - 1, 1, f], dev(k, (z + 1) % 4), has_right)
+        if both:
+            start(("col", b, f0, -1), cols.at[b - 1, 0, f], cols_in.at[b - 1, 0, f], dev(k, (z + 3) % 4), has_left)
+        for dk, dz in directions(both):
+            c = (dk > 0) * 2 + (dz > 0)
+            ok = (has_down if dk > 0 else has_up) & (has_right if dz > 0 else has_left)
+            start(
+                ("corner", b, f0, dk, dz), corners.at[b - 1, c, f], corners_in.at[b - 1, c, f],
+                dev((k + dk) % 16, (z + dz) % 4), ok,
+            )
+
+    def edges_arrived(b, f0, nf, both=True):
+        f = pl.ds(f0, nf)
+        rows_arrived(b, f0, nf, inner, both)
+        arrived(("col", b, f0, 1), cols_in.at[b - 1, 1, f], has_left)
+        if both:
+            arrived(("col", b, f0, -1), cols_in.at[b - 1, 0, f], has_right)
+
+        @pl.when(has_left)
+        def _():
+            for fr in range(f0, f0 + nf):
+                padded[b, fr, 1:9, LEFT : LEFT + 1, :] = cols_in[b - 1, 1, fr]
+
+        if both:
+            @pl.when(has_right)
+            def _():
+                for fr in range(f0, f0 + nf):
+                    padded[b, fr, 1:9, RIGHT : RIGHT + 1, :] = cols_in[b - 1, 0, fr]
+
+        for dk, dz in directions(both):
+            c = (dk > 0) * 2 + (dz > 0)
+            ok = (has_up if dk > 0 else has_down) & (has_left if dz > 0 else has_right)
+            arrived(("corner", b, f0, dk, dz), corners_in.at[b - 1, c, f], ok)
+
+            @pl.when(ok)
+            def _():
+                row, col = 0 if dk > 0 else 9, LEFT if dz > 0 else RIGHT
+                for fr in range(f0, f0 + nf):
+                    padded[b, fr, row, col : col + 1, :] = corners_in[b - 1, c, fr]
+
+    def conv(b, fr):
+        at = fr % 2
+        for dx in range(3):
+            window = padded[b, fr, :, LEFT + dx : LEFT + dx + 40, :]
+            for dy in range(3):
+                lanes = slice((dy * 3 + dx) * 128, (dy * 3 + dx) * 128 + 128)
+                high, low = split(window[dy : dy + 8].reshape(320, 128))
+                a_hi[at, :, lanes] = high
+                a_lo[at, :, lanes] = low
+        mixed = two_part(a_hi[at], a_lo[at], w_space[b])
+        u = act(mixed, gain_ref[b, 1:2, :])
+        put(fr, u)
+        if fr >= 2:
+            late[b, fr - 2] = u
+            start(
+                ("late", b, fr), late.at[b, fr - 2], late_in.at[b, fr - 2],
+                dev(k, z, (frame + 1) % 4), frame < 3,
+            )
+
+    def put(fr, u):
+        lanes = slice((fr + 2) * 128, (fr + 3) * 128)
+        u_hi[:, lanes], u_lo[:, lanes] = split(u)
+
+    def earlier(b):
+        for fr in (2, 3):
+            arrived(("late", b, fr), late_in.at[b, fr - 2], frame > 0)
+
+        @pl.when(frame > 0)
+        def _():
+            put(-2, late_in[b, 0])
+            put(-1, late_in[b, 1])
+
+        @pl.when(frame == 0)
+        def _():
+            for parts in (u_hi, u_lo):
+                parts[:, 0:128] = parts[:, 256:384]
+                parts[:, 128:256] = parts[:, 256:384]
+
+    def mix(b, fr):
+        lanes = slice(fr * 128, fr * 128 + 384)
+        return state[fr].reshape(320, 128) + two_part(u_hi[:, lanes], u_lo[:, lanes], w_time[b])
+
+    for dz in range(1, 4):
+        arrived(("ext", dz), ext_in.at[(z + dz) % 4])
+    gain = gain_ref[0, 0:1, :]
+    for fr in order:
+        for dz in range(1, 4):
+            arrived(("band", fr, dz), state.at[fr, pl.ds(((z + dz) % 4) * 2, 2)])
+        padded[0, fr, 1:9, 8:48, :] = act(state[fr].reshape(320, 128), gain).reshape(8, 40, 128)
+        for src in range(4):
+            fringe = act(ext_in[src, fr], gain)
+            rows = slice(1 + 2 * src, 3 + 2 * src)
+
+            @pl.when(has_left)
+            def _():
+                padded[0, fr, rows, LEFT : LEFT + 1, :] = fringe[0:2]
+
+            @pl.when(has_right)
+            def _():
+                padded[0, fr, rows, RIGHT : RIGHT + 1, :] = fringe[2:4]
+        send_rows(0, fr, 1, slice(None))
+    for fr in order:
+        rows_arrived(0, fr, 1, slice(None))
+        conv(0, fr)
+
+    gain = gain_ref[1, 0:1, :]
+    for f0 in (2, 0):
+        if f0 == 0:
+            earlier(0)
+        for fr in (f0, f0 + 1):
+            x = mix(0, fr)
+            padded[1, fr, 1:9, 8:48, :] = act(x, gain).reshape(8, 40, 128)
+            late_x = x.reshape(8, 40, 128)
+            state[fr] = late_x
+        send_rows(1, f0, 2, inner)
+        send_edges(1, f0, 2)
+    for f0 in (2, 0):
+        edges_arrived(1, f0, 2)
+        for fr in (f0, f0 + 1):
+            conv(1, fr)
+    for f0 in (2, 0):
+        if f0 == 0:
+            earlier(1)
+        for fr in (f0, f0 + 1):
+            padded[2, fr, 1:9, 8:48, :] = mix(1, fr).reshape(8, 40, 128)
+        send_rows(2, f0, 2, inner, False)
+        send_edges(2, f0, 2, False)
+
+    for f0 in (2, 0):
+        edges_arrived(2, f0, 2, False)
+        for fr in (f0, f0 + 1):
+            for row in range(4):
+                at = slice((fr - f0) * 96 + row * 24, (fr - f0) * 96 + row * 24 + 24)
+                for dy in range(3):
+                    for dx in range(3):
+                        taken = padded[2, fr, 2 * row + dy, pl.ds(LEFT + dx, 24, stride=2), :]
+                        lanes = slice((dy * 3 + dx) * 128, (dy * 3 + dx) * 128 + 128)
+                        high = taken.astype(BF16).astype(F32)
+                        d_hi[at, lanes] = high
+                        d_lo[at, lanes] = taken - high
+        high, low = d_hi[...].astype(BF16), d_lo[...].astype(BF16)
+        lowered = jnp.dot(high, w_hi[...], preferred_element_type=F32)
+        lowered = lowered + jnp.dot(high, w_lo[...], preferred_element_type=F32)
+        lowered = lowered + jnp.dot(low, w_hi[...], preferred_element_type=F32)
+        for fr in (f0, f0 + 1):
+            for row in range(4):
+                for part in range(4):
+                    at = (fr - f0) * 96 + row * 24 + part * 5
+                    out_ref[fr, part * 20 + row * 5 : part * 20 + row * 5 + 5, :] = lowered[at : at + 5]
+
+    for copy, cond in sent:
+        when(cond, copy.wait_send)
+
+
+def conv_all(video, norm_gain, space_weight, time_weight, down_weight):
+    vmem = pl.BlockSpec(memory_space=pltpu.VMEM)
+    dma = pltpu.SemaphoreType.DMA
+    return pl.pallas_call(
+        conv_kernel,
+        out_shape=jax.ShapeDtypeStruct((4, 80, 256), F32),
+        in_specs=[vmem] * 5,
+        out_specs=vmem,
+        scratch_shapes=[
+            pltpu.VMEM((4, 8, 40, 128), F32),
+            pltpu.VMEM((3, 4, 10, 56, 128), F32),
+            pltpu.VMEM((4, 4, 4, 1, 128), F32),
+            pltpu.VMEM((4, 4, 4, 1, 128), F32),
+            pltpu.VMEM((2, 2, 4, 8, 1, 128), F32),
+            pltpu.VMEM((2, 2, 4, 8, 1, 128), F32),
+            pltpu.VMEM((2, 4, 4, 1, 128), F32),
+            pltpu.VMEM((2, 4, 4, 1, 128), F32),
+            pltpu.VMEM((2, 2, 320, 128), F32),
+            pltpu.VMEM((2, 2, 320, 128), F32),
+            pltpu.VMEM((320, 768), BF16),
+            pltpu.VMEM((320, 768), BF16),
+            pltpu.VMEM((2, 320, 1152), BF16),
+            pltpu.VMEM((2, 320, 1152), BF16),
+            pltpu.VMEM((192, 1152), F32),
+            pltpu.VMEM((192, 1152), F32),
+            pltpu.VMEM((2, 1152, 256), BF16),
+            pltpu.VMEM((2, 384, 256), BF16),
+            pltpu.VMEM((1152, 256), BF16),
+            pltpu.VMEM((1152, 256), BF16),
+            dma((64,)), dma((64,)),
+        ],
+        compiler_params=pltpu.CompilerParams(
+            collective_id=2, has_side_effects=True, vmem_limit_bytes=48 * 2**20
+        ),
+        name="blocks",
+    )(
+        video, norm_gain, space_weight.reshape(2, 1152, 128), time_weight.reshape(2, 384, 128),
+        down_weight.reshape(1152, 256),
+    )
 
 
 def three_pass(a, b):
@@ -82,9 +378,6 @@
 
 def dot_f32(a, b, dims=((1,), (0,))):
     return lax.dot_general(a, b, (dims, ((), ())), precision=highest, preferred_element_type=F32)
-
-
-QT = 128
 
 
 def attend_kernel(
@@ -107,8 +400,6 @@
     sibling = dev(x, y, z, 1 - core)
     sz = 2 * core + s
     crossed = half != core
-    idx = y * 4 + sz
-    me_q = y * 4 + z
 
     barrier = pltpu.get_barrier_semaphore()
 
@@ -124,14 +415,15 @@
     def _():
         hello(dev(x, y, sz, half))
 
-    for k in range(16):
-        sy, ssz, sc = k // 4, 2 * core + (k % 2), (k // 2) % 2
-
-        @pl.when(jnp.logical_not((sy == y) & (ssz == z) & (sc == core)))
-        def _():
-            hello(dev(x, sy, ssz, sc))
-
-    pl.semaphore_wait(barrier, 22 + 2 * crossed.astype(jnp.int32))
+    from_z, from_core = 2 * core + y % 2, y // 2
+    expected = 7 + crossed.astype(jnp.int32)
+    for j in range(4):
+        @pl.when(jnp.logical_not((j == y) & (from_z == z) & (from_core == core)))
+        def _():
+            hello(dev(x, j, from_z, from_core))
+
+        expected = expected + jnp.logical_not((sz == y) & (z == j) & (half == core)).astype(jnp.int32)
+    pl.semaphore_wait(barrier, expected)
 
     slot = s * 4 + y
     first = []
@@ -212,20 +504,15 @@
     def attend(block, which):
         normed[...] = norm(keys[block], gain)
 
-        def tile_step(t, _):
-            rows = pl.ds(pl.multiple_of(t * 64, 64), 64)
-            k = normed[...]
-            scores = dot_f32(query[which, rows, :], k, ((1,), (1,)))
-            old = best[which, rows, :]
-            new = jnp.maximum(old, jnp.max(scores, axis=1, keepdims=True))
-            factor = jnp.exp(old - new)
-            weights = jnp.exp(scores - new)
-            total[which, rows, :] = total[which, rows, :] * factor + jnp.sum(weights, axis=1, keepdims=True)
-            best[which, rows, :] = new
-            acc[which, rows, :] = acc[which, rows, :] * factor + three_pass(weights, k)
-            return 0
-
-        lax.fori_loop(0, 5, tile_step, 0)
+        k = normed[...]
+        scores = dot_f32(query[which], k, ((1,), (1,)))
+        old = best[which]
+        new = jnp.maximum(old, jnp.max(scores, axis=1, keepdims=True))
+        factor = jnp.exp(old - new)
+        weights = jnp.exp(scores - new)
+        total[which] = total[which] * factor + jnp.sum(weights, axis=1, keepdims=True)
+        best[which] = new
+        acc[which] = acc[which] * factor + three_pass(weights, k)
 
     def attend_both(block):
         attend(block, 1)
@@ -275,33 +562,31 @@
     mixed = (acc[0] * mine_f + part_acc[...] * other_f) / whole
     value = dot_f32(mixed, wv_ref[...])
     y_out = keys[slot] + dot_f32(value, wo_ref[...])
-    for q in range(16):
+    for part in range(4):
         for b in range(4):
-            start = b * 80 + q * 5
-            result[q, b] = y_out[start : start + 5]
+            start = b * 80 + part * 20
+            result[part, b] = y_out[start : start + 20]
 
     backs = []
-    for k in range(16):
-        q = (me_q + k) % 16
+    for part in range(4):
         copy = pltpu.make_async_remote_copy(
-            src_ref=result.at[q],
-            dst_ref=out_ref.at[:, idx],
-            send_sem=rets.at[k],
-            recv_sem=retr.at[idx],
-            device_id=dev(x, q // 4, q % 4, half),
+            src_ref=result.at[part],
+            dst_ref=out_ref.at[:, y],
+            send_sem=rets.at[part],
+            recv_sem=retr.at[y],
+            device_id=dev(x, sz, part, half),
             device_id_type=MESH,
         )
-        backs.append(copy)
-        if k > 0:
+        stays = (sz == y) & (z == part) & (half == core)
+        backs.append((copy, stays))
+
+        @pl.when(jnp.logical_not(stays))
+        def _():
             copy.start()
 
-    @pl.when(crossed)
-    def _():
-        backs[0].start()
-
-    @pl.when(jnp.logical_not(crossed))
-    def _():
-        out_ref[:, pl.ds(idx, 1), :, :] = result[me_q][:, None]
+        @pl.when(stays)
+        def _():
+            out_ref[:, pl.ds(y, 1), :, :] = result[part][:, None]
 
     for copy in first:
         copy.wait_send()
@@ -309,22 +594,23 @@
     @pl.when(crossed)
     def _():
         cross.wait_send()
-        backs[0].wait_send()
 
     for copy in sent:
         copy.wait_send()
-    for k in range(16):
-        if k > 0:
-            backs[k].wait_send()
-        sy, ssz, sc = k // 4, 2 * core + (k % 2), (k // 2) % 2
-
-        @pl.when(jnp.logical_not((sy == y) & (ssz == z) & (sc == core)))
+    for copy, stays in backs:
+        @pl.when(jnp.logical_not(stays))
+        def _():
+            copy.wait_send()
+    for sy in range(4):
+        here = (sy == y) & (z == 2 * core + y % 2) & (core == y // 2)
+
+        @pl.when(jnp.logical_not(here))
         def _():
             pltpu.make_async_remote_copy(
                 src_ref=result.at[0],
-                dst_ref=out_ref.at[:, k],
-                send_sem=rets.at[k],
-                recv_sem=retr.at[k],
+                dst_ref=out_ref.at[:, sy],
+                send_sem=rets.at[0],
+                recv_sem=retr.at[sy],
                 device_id=sibling,
                 device_id_type=MESH,
             ).wait_recv()
@@ -335,7 +621,7 @@
     dma = pltpu.SemaphoreType.DMA
     out = pl.pallas_call(
         attend_kernel,
-        out_shape=jax.ShapeDtypeStruct((4, 16, 5, 256), F32),
+        out_shape=jax.ShapeDtypeStruct((4, 4, 20, 256), F32),
         in_specs=[vmem] * 6,
         out_specs=vmem,
         scratch_shapes=[
@@ -347,8 +633,8 @@
             pltpu.VMEM((320, 256), F32),
             pltpu.VMEM((320, 256), F32),
             pltpu.VMEM((2, 2, 320, 128), F32),
-            pltpu.VMEM((16, 4, 5, 256), F32),
-            dma((4,)), dma((4,)), dma((11,)), dma((11,)), dma((16,)), dma((16,)),
+            pltpu.VMEM((4, 4, 20, 256), F32),
+            dma((4,)), dma((4,)), dma((11,)), dma((11,)), dma((4,)), dma((4,)),
         ],
         compiler_params=pltpu.CompilerParams(
             collective_id=1, has_side_effects=True, vmem_limit_bytes=40 * 2**20
@@ -370,22 +656,7 @@
     w_value,
     w_out,
 ):
-    state = video
-    for block in range(2):
-        wide = extended(act(state, norm_gain[block, 0]), (("tile", 1),), 1)
-        mixed = conv_rows(wide, space_weight[block])
-        state = state + time_mix(act(mixed, norm_gain[block, 1]), time_weight[block])
-    upper = passed_along(state[:, -1:], "tile", 1)
-    stacked = jnp.concatenate([upper, state], 1)
-    lowered = lax.conv_general_dilated(
-        stacked,
-        down_weight,
-        (2, 2),
-        ((0, 0), (1, 0)),
-        dimension_numbers=("NHWC", "HWIO", "NHWC"),
-        precision=highest,
-    )
-    lowered = lowered.reshape(4, 80, 256)
+    lowered = conv_all(video, norm_gain, space_weight, time_weight, down_weight)
     return attend_all(lowered, attn_gain, w_query, w_key, w_value, w_out)
 
 

time: 211 us -> 107 us (0.51)
  waiting for transfers between devices: 50.1 us -> 0 us
  starting transfers between devices: 28.3 us -> 0 us
  matrix products: 22.3 us -> 0 us
  other arithmetic: 3.97 us -> 0 us
  local copies, waits for them, and re-layouts: 2.15 us -> 6.08 us
    ppermute x7 -> x0, waiting for transfers between devices: 50.1 us -> none  [the longest x3 28 us: passed_along(): return lax.ppermute(shard, axis, pairs)]
    ppermute x7 -> x0, starting transfers between devices: 28.3 us -> none  [the longest x2 12.5 us: extended(): lax.ppermute(tail, axis, [(i, (i + 1) % count) for i in range(ends)])]
    conv_general_dilated x3 -> x0, matrix products: 18.1 us -> none  [the longest x2 14.9 us: conv_rows(): lax.conv_general_dilated(inputs, kernel, (1, 1), ((0, 0), (1, 1)), dimens...]
    unnamed x20, local copies, waits for them, and re-layouts: 0.06 us -> 5.32 us
    dot_general x6 -> x0, matrix products: 4.21 us -> none  [the longest x2 1.56 us: time_mix(): jnp.einsum('fhwc,cd->fhwd', padded[0:count], kernel[0], precision=highest)]
    mul x4 -> x0, other arithmetic: 2.13 us -> none  [act(): return jax.nn.silu(norm(values, gain))]
    pallas_call x1 -> x2, Pallas kernels: 103 us -> 101 us  [the longest x1 58.3 us: attend_all(): pl.pallas_call(attend_kernel, out_shape=jax.ShapeDtypeStruct((4, 4, 20, 2...]
  transfers between devices with their start and end apart: 7 -> 0, of which waited for: 7 -> 0; matrix products, arithmetic and copies ran while one was open for 1% -> 0% of each run, Pallas kernels for 0% -> 0%
where the time goes in v1:
time: 107 us
  Pallas kernels  101 us (94%)
  local copies, waits for them, and re-layouts  6.08 us (6%)
    pallas_call x1, Pallas kernels, attend_all(): pl.pallas_call(attend_kernel, out_shape=jax.ShapeDtypeStruct((4, 4, 20, 2...  58.3 us
    pallas_call x1, Pallas kernels, conv_all(): pl.pallas_call(conv_kernel, out_shape=jax.ShapeDtypeStruct((4, 80, 256),...  42.6 us
    unnamed x20, local copies, waits for them, and re-layouts  5.32 us

profile of v1, /device:TPU:232, one launch (start us, length us, event | category | flops | bytes accessed | tf_op | source)
XLA Modules:
  0.0 107.0 jit_solution(4120362841947495372)
XLA Ops:
  0.0 0.0 copy-start
  0.0 1.3 %copy-done = f32[2,3,3,128,128]{4,3,2,1,0:T(8,128)S(1)} copy-done((f32[2,3,3,128,128]{4,3,2,1,0:T(8,128)S(1)}, f32[2,3,3,128,128]{4,3,2,1,0:T(8,128)}, u32[]{:S(2)}) %copy-start) | copy-done | bytes 1179672
  1.3 0.0 copy-start.1
  1.3 1.3 %copy-done.1 = f32[3,3,128,256]{3,2,1,0:T(8,128)S(1)} copy-done((f32[3,3,128,256]{3,2,1,0:T(8,128)S(1)}, f32[3,3,128,256]{3,2,1,0:T(8,128)}, u32[]{:S(2)}) %copy-start.1) | copy-done | bytes 1179672
  2.5 0.0 copy-start.2
  2.5 1.1 %copy-done.2 = f32[4,2,160,128]{3,2,1,0:T(8,128)S(1)} copy-done((f32[4,2,160,128]{3,2,1,0:T(8,128)S(1)}, f32[4,2,160,128]{3,2,1,0:T(8,128)}, u32[]{:S(2)}) %copy-start.2) | copy-done | bytes 655384
  3.6 0.0 copy-start.3
  3.6 1.0 copy-done.3
  4.6 0.0 copy-start.8
  4.6 0.7 copy-done.8
  5.3 0.0 copy-start.4
  5.3 0.0 copy-start.5
  5.3 0.0 copy-start.6
  5.3 0.0 copy-start.7
  5.3 0.0 copy-start.9
  5.3 42.6 %blocks.1.z_ref = f32[4,80,256]{2,1,0:T(8,128)S(1)} custom-call(f32[4,2,160,128]{3,2,1,0:T(8,128)S(1)} %copy-done.2, f32[2,2,128]{2,1,0:T(2,128)S(1)} %copy-done.8, f32[2,1152,128]{2,1,0:T(8,128)S(1)} %bitcast.4, f32[2,384,128]{2,1,0:T(8,128)S(1)} %bitcast.6, f32[1152,256]{1,0:T(8,128)S(1)} %bitcast.5), custom_call_target="tpu_custom_call" | custom-call | tf_op jit(solution)/shard_map/blocks/pallas_call | solution.py:333
  47.9 0.0 copy-done.4
  48.0 0.0 copy-done.5
  48.0 0.0 copy-done.6
  48.0 0.0 copy-done.7
  48.0 0.0 copy-done.9
  48.0 58.3 %attend.1 = f32[4,4,20,256]{3,2,1,0:T(8,128)S(1)} custom-call(f32[4,80,256]{2,1,0:T(8,128)S(1)} %blocks.1.z_ref, f32[1,256]{1,0:T(1,128)S(1)} %bitcast.7, f32[256,256]{1,0:T(8,128)S(1)} %copy-done.4, f32[256,256]{1,0:T(8,128)S(1)} %copy-done.5, f32[256,256]{1,0:T(8,128)S(1)} %copy-done.6, f32[256,256]{1,0:T(8,128)S(1)} %copy-done.7), custom_call_target="tpu_custom_call" | custom-call | tf_op jit(solution)/shard_map/attend/pallas_call | solution.py:622
  106.3 0.8 reshape.19
Async XLA Ops:
  0.0 1.3 %copy-start = (f32[2,3,3,128,128]{4,3,2,1,0:T(8,128)S(1)}, f32[2,3,3,128,128]{4,3,2,1,0:T(8,128)}, u32[]{:S(2)}) copy-start(f32[2,3,3,128,128]{4,3,2,1,0:T(8,128)} %param.12) | copy-start | bytes 3538948
  1.3 1.3 %copy-start.1 = (f32[3,3,128,256]{3,2,1,0:T(8,128)S(1)}, f32[3,3,128,256]{3,2,1,0:T(8,128)}, u32[]{:S(2)}) copy-start(f32[3,3,128,256]{3,2,1,0:T(8,128)} %param.14) | copy-start | bytes 3538948
  2.5 1.1 %copy-start.2 = (f32[4,2,160,128]{3,2,1,0:T(8,128)S(1)}, f32[4,2,160,128]{3,2,1,0:T(8,128)}, u32[]{:S(2)}) copy-start(f32[4,2,160,128]{3,2,1,0:T(8,128)} %video_ref.1) | copy-start | bytes 1966084
  3.6 1.0 copy-start.3
  4.6 0.7 copy-start.8
  5.3 42.6 %copy-start.4 = (f32[256,256]{1,0:T(8,128)S(1)}, f32[256,256]{1,0:T(8,128)}, u32[]{:S(2)}) copy-start(f32[256,256]{1,0:T(8,128)} %wq_ref.1) | copy-start | bytes 786436
  5.3 42.6 %copy-start.5 = (f32[256,256]{1,0:T(8,128)S(1)}, f32[256,256]{1,0:T(8,128)}, u32[]{:S(2)}) copy-start(f32[256,256]{1,0:T(8,128)} %wk_ref.1) | copy-start | bytes 786436
  5.3 42.6 %copy-start.6 = (f32[256,256]{1,0:T(8,128)S(1)}, f32[256,256]{1,0:T(8,128)}, u32[]{:S(2)}) copy-start(f32[256,256]{1,0:T(8,128)} %wv_ref.1) | copy-start | bytes 786436
  5.3 42.7 %copy-start.7 = (f32[256,256]{1,0:T(8,128)S(1)}, f32[256,256]{1,0:T(8,128)}, u32[]{:S(2)}) copy-start(f32[256,256]{1,0:T(8,128)} %wo_ref.1) | copy-start | bytes 786436
  5.3 42.7 %copy-start.9 = (f32[256]{0:T(256)S(1)}, f32[256]{0:T(256)}, u32[]{:S(2)}) copy-start(f32[256]{0:T(256)} %param.15) | copy-start | bytes 3076

commit v2 on v1

v2 whole, which is shorter than its diff:
```python
import jax
import jax.numpy as jnp
from jax import lax
from jax.experimental import pallas as pl
from jax.experimental.pallas import tpu as pltpu
from jax.sharding import PartitionSpec as P

highest = lax.Precision.HIGHEST
MESH = pl.DeviceIdType.MESH
F32 = jnp.float32
BF16 = jnp.bfloat16


def norm(values, gain):
    return values * lax.rsqrt(jnp.mean(values * values, -1, keepdims=True) + 1e-06) * gain


def split(values):
    high = values.astype(BF16)
    return high, (values - high.astype(F32)).astype(BF16)


LEFT, RIGHT = 7, 48


def act(values, gain):
    scaled = values * lax.rsqrt(jnp.mean(values * values, -1, keepdims=True) + 1e-06) * gain
    return scaled / (1.0 + jnp.exp(-scaled))


def conv_part(
    video_hbm, space_hbm, time_hbm, down_hbm, gain_ref, z_ref,
    video_ref, space_ref, time_ref, down_ref,
    state, padded, ext, ext_in, cols, cols_in, corners, corners_in,
    late, late_in, u_hi, u_lo, a_hi, a_lo, d_hi, d_lo, w_space, w_time, w_hi, w_lo,
    send_sems, recv_sems, load_sems, greet, lowered_ready,
):
    tile = lax.axis_index("tile")
    frame = lax.axis_index("frame")
    loads = [
        pltpu.make_async_copy(video_hbm, video_ref, load_sems.at[0]),
        pltpu.make_async_copy(space_hbm, space_ref, load_sems.at[1]),
        pltpu.make_async_copy(time_hbm, time_ref, load_sems.at[2]),
        pltpu.make_async_copy(down_hbm, down_ref, load_sems.at[3]),
    ]
    for load in loads:
        load.start()
    k, z = tile // 4, tile % 4
    has_up, has_down = k > 0, k < 15
    has_left, has_right = z > 0, z < 3

    def dev(k, z, frame=frame):
        return {"tile": k * 4 + z, "frame": frame}

    def when(cond, fn):
        if cond is None:
            fn()
        else:
            pl.when(cond)(fn)

    ids = {}
    sent = []

    def message(name, src, dst, device):
        i = ids.setdefault(name, len(ids))
        return pltpu.make_async_remote_copy(
            src_ref=src, dst_ref=dst, send_sem=send_sems.at[i], recv_sem=recv_sems.at[i],
            device_id=device, device_id_type=MESH,
        )

    def start(name, src, dst, device, cond=None):
        copy = message(name, src, dst, device)
        when(cond, copy.start)
        sent.append((copy, cond))

    def arrived(name, ref, cond=None):
        copy = message(name, ref, ref, dev(k, (z + 1) % 4))
        when(cond, copy.wait_recv)

    for b in range(3):
        padded[b, :, :, 0:8, :] = jnp.zeros((4, 10, 8, 128), F32)
        padded[b, :, :, 48:56, :] = jnp.zeros((4, 10, 8, 128), F32)

        @pl.when(jnp.logical_not(has_up))
        def _():
            padded[b, :, 0, :, :] = jnp.zeros((4, 56, 128), F32)

        @pl.when(jnp.logical_not(has_down))
        def _():
            padded[b, :, 9, :, :] = jnp.zeros((4, 56, 128), F32)

    barrier = pltpu.get_barrier_semaphore()

    def hello(device, cond=None):
        when(cond, lambda: pl.semaphore_signal(barrier, inc=1, device_id=device, device_id_type=MESH))

    sides = ((-1, has_up), (1, has_down))
    flanks = ((-1, has_left), (1, has_right))
    for dz in range(1, 4):
        hello(dev(k, (z + dz) % 4))
    for dk, ok in sides:
        hello(dev((k + dk) % 16, z), ok)
        for dz, fine in flanks:
            hello(dev((k + dk) % 16, (z + dz) % 4), ok & fine)
    hello(dev(k, z, (frame + 3) % 4), frame > 0)
    count = 3 + (frame < 3).astype(jnp.int32)
    across = 1 + has_left.astype(jnp.int32) + has_right.astype(jnp.int32)
    count = count + (has_up.astype(jnp.int32) + has_down.astype(jnp.int32)) * across
    pl.semaphore_wait(barrier, count + greet(hello))

    order = (2, 3, 0, 1)

    def band(part):
        return pl.ds(pl.multiple_of(part * 40, 8), 40)

    for fr in order:
        for dz in (2, 1, 3):
            part = (z + dz) % 4
            start(("band", fr, dz), video_hbm.at[fr, :, band(part), :], state.at[fr, pl.ds(z * 2, 2)], dev(k, part))
    loads[0].wait()
    for part in range(4):
        for fr in range(4):
            if part == 0:
                ext[part, fr, 0:2] = jnp.zeros((2, 1, 128), F32)
            else:
                ext[part, fr, 0:2] = video_ref[fr, :, 40 * part - 1 : 40 * part, :]
            if part == 3:
                ext[part, fr, 2:4] = jnp.zeros((2, 1, 128), F32)
            else:
                ext[part, fr, 2:4] = video_ref[fr, :, 40 * part + 40 : 40 * part + 41, :]

    for dz in (2, 1, 3):
        part = (z + dz) % 4
        start(("ext", dz), ext.at[part], ext_in.at[z], dev(k, part))
    ext_in[z] = ext[z]
    for fr in range(4):
        state[fr, pl.ds(z * 2, 2)] = video_ref[fr, :, band(z), :]

    for load in loads[1:]:
        load.wait()
    for b in range(2):
        for tap in range(9):
            rows = slice(tap * 128, tap * 128 + 128)
            high, low = split(space_ref[b, rows, :])
            w_space[b, rows, 0:128] = high
            w_space[b, rows, 128:256] = low
        high, low = split(time_ref[b])
        w_time[b, :, 0:128] = high
        w_time[b, :, 128:256] = low
    for tap in range(9):
        rows = slice(tap * 128, tap * 128 + 128)
        high, low = split(down_ref[rows, :])
        w_hi[rows, :] = high
        w_lo[rows, :] = low

    def two_part(high, low, weight):
        both = jnp.dot(high, weight, preferred_element_type=F32)
        rest = jnp.dot(low, weight[:, 0:128], preferred_element_type=F32)
        return both[:, 0:128] + both[:, 128:256] + rest

    inner = pl.ds(8, 40)

    def send_rows(b, f0, nf, width, both=True):
        f = pl.ds(f0, nf)
        start(("row", b, f0, 1), padded.at[b, f, 8, width, :], padded.at[b, f, 0, width, :], dev((k + 1) % 16, z), has_down)
        if both:
            start(("row", b, f0, -1), padded.at[b, f, 1, width, :], padded.at[b, f, 9, width, :], dev((k + 15) % 16, z), has_up)

    def rows_arrived(b, f0, nf, width, both=True):
        f = pl.ds(f0, nf)
        arrived(("row", b, f0, 1), padded.at[b, f, 0, width, :], has_up)
        if both:
            arrived(("row", b, f0, -1), padded.at[b, f, 9, width, :], has_down)

    def directions(both):
        return ((1, 1), (1, -1), (-1, 1), (-1, -1)) if both else ((1, 1),)

    def send_edges(b, f0, nf, both=True):
        f = pl.ds(f0, nf)
        for fr in range(f0, f0 + nf):
            cols[b - 1, 1, fr] = padded[b, fr, 1:9, 47:48, :]
            if both:
                cols[b - 1, 0, fr] = padded[b, fr, 1:9, 8:9, :]
            for dk, dz in directions(both):
                row, col = 8 if dk > 0 else 1, 47 if dz > 0 else 8
                corners[b - 1, (dk > 0) * 2 + (dz > 0), fr] = padded[b, fr, row, col : col + 1, :]
        start(("col", b, f0, 1), cols.at[b - 1, 1, f], cols_in.at[b - 1, 1, f], dev(k, (z + 1) % 4), has_right)
        if both:
            start(("col", b, f0, -1), cols.at[b - 1, 0, f], cols_in.at[b - 1, 0, f], dev(k, (z + 3) % 4), has_left)
        for dk, dz in directions(both):
            c = (dk > 0) * 2 + (dz > 0)
            ok = (has_down if dk > 0 else has_up) & (has_right if dz > 0 else has_left)
            start(
                ("corner", b, f0, dk, dz), corners.at[b - 1, c, f], corners_in.at[b - 1, c, f],
                dev((k + dk) % 16, (z + dz) % 4), ok,
            )

    def edges_arrived(b, f0, nf, both=True):
        f = pl.ds(f0, nf)
        rows_arrived(b, f0, nf, inner, both)
        arrived(("col", b, f0, 1), cols_in.at[b - 1, 1, f], has_left)
        if both:
            arrived(("col", b, f0, -1), cols_in.at[b - 1, 0, f], has_right)

        @pl.when(has_left)
        def _():
            for fr in range(f0, f0 + nf):
                padded[b, fr, 1:9, LEFT : LEFT + 1, :] = cols_in[b - 1, 1, fr]

        if both:
            @pl.when(has_right)
            def _():
                for fr in range(f0, f0 + nf):
                    padded[b, fr, 1:9, RIGHT : RIGHT + 1, :] = cols_in[b - 1, 0, fr]

        for dk, dz in directions(both):
            c = (dk > 0) * 2 + (dz > 0)
            ok = (has_up if dk > 0 else has_down) & (has_left if dz > 0 else has_right)
            arrived(("corner", b, f0, dk, dz), corners_in.at[b - 1, c, f], ok)

            @pl.when(ok)
            def _():
                row, col = 0 if dk > 0 else 9, LEFT if dz > 0 else RIGHT
                for fr in range(f0, f0 + nf):
                    padded[b, fr, row, col : col + 1, :] = corners_in[b - 1, c, fr]

    def conv(b, fr):
        at = fr % 2
        for dx in range(3):
            window = padded[b, fr, :, LEFT + dx : LEFT + dx + 40, :]
            for dy in range(3):
                lanes = slice((dy * 3 + dx) * 128, (dy * 3 + dx) * 128 + 128)
                high, low = split(window[dy : dy + 8].reshape(320, 128))
                a_hi[at, :, lanes] = high
                a_lo[at, :, lanes] = low
        mixed = two_part(a_hi[at], a_lo[at], w_space[b])
        u = act(mixed, gain_ref[b, 1:2, :])
        put(fr, u)
        if fr >= 2:
            late[b, fr - 2] = u
            start(
                ("late", b, fr), late.at[b, fr - 2], late_in.at[b, fr - 2],
                dev(k, z, (frame + 1) % 4), frame < 3,
            )

    def put(fr, u):
        lanes = slice((fr + 2) * 128, (fr + 3) * 128)
        u_hi[:, lanes], u_lo[:, lanes] = split(u)

    def earlier(b):
        for fr in (2, 3):
            arrived(("late", b, fr), late_in.at[b, fr - 2], frame > 0)

        @pl.when(frame > 0)
        def _():
            put(-2, late_in[b, 0])
            put(-1, late_in[b, 1])

        @pl.when(frame == 0)
        def _():
            for parts in (u_hi, u_lo):
                parts[:, 0:128] = parts[:, 256:384]
                parts[:, 128:256] = parts[:, 256:384]

    def mix(b, fr):
        lanes = slice(fr * 128, fr * 128 + 384)
        return state[fr].reshape(320, 128) + two_part(u_hi[:, lanes], u_lo[:, lanes], w_time[b])

    for dz in range(1, 4):
        arrived(("ext", dz), ext_in.at[(z + dz) % 4])
    gain = gain_ref[0, 0:1, :]
    for at, fr in enumerate(order):
        for dz in range(1, 4):
            arrived(("band", fr, dz), state.at[fr, pl.ds(((z + dz) % 4) * 2, 2)])
        padded[0, fr, 1:9, 8:48, :] = act(state[fr].reshape(320, 128), gain).reshape(8, 40, 128)
        for src in range(4):
            fringe = act(ext_in[src, fr], gain)
            rows = slice(1 + 2 * src, 3 + 2 * src)

            @pl.when(has_left)
            def _():
                padded[0, fr, rows, LEFT : LEFT + 1, :] = fringe[0:2]

            @pl.when(has_right)
            def _():
                padded[0, fr, rows, RIGHT : RIGHT + 1, :] = fringe[2:4]
        send_rows(0, fr, 1, slice(None))
        if at > 0:
            rows_arrived(0, order[at - 1], 1, slice(None))
            conv(0, order[at - 1])
    rows_arrived(0, order[3], 1, slice(None))
    conv(0, order[3])

    gain = gain_ref[1, 0:1, :]

    def middle(f0):
        for fr in (f0, f0 + 1):
            x = mix(0, fr)
            padded[1, fr, 1:9, 8:48, :] = act(x, gain).reshape(8, 40, 128)
            state[fr] = x.reshape(8, 40, 128)
        send_rows(1, f0, 2, inner)
        send_edges(1, f0, 2)

    middle(2)
    edges_arrived(1, 2, 2)
    for fr in (2, 3):
        conv(1, fr)
    earlier(0)
    middle(0)
    edges_arrived(1, 0, 2)
    for fr in (0, 1):
        conv(1, fr)
    for f0 in (2, 0):
        if f0 == 0:
            earlier(1)
        for fr in (f0, f0 + 1):
            padded[2, fr, 1:9, 8:48, :] = mix(1, fr).reshape(8, 40, 128)
        send_rows(2, f0, 2, inner, False)
        send_edges(2, f0, 2, False)

    for f0 in (2, 0):
        edges_arrived(2, f0, 2, False)
        for fr in (f0, f0 + 1):
            for row in range(4):
                at = slice((fr - f0) * 96 + row * 24, (fr - f0) * 96 + row * 24 + 24)
                for dy in range(3):
                    for dx in range(3):
                        taken = padded[2, fr, 2 * row + dy, pl.ds(LEFT + dx, 24, stride=2), :]
                        lanes = slice((dy * 3 + dx) * 128, (dy * 3 + dx) * 128 + 128)
                        high = taken.astype(BF16).astype(F32)
                        d_hi[at, lanes] = high
                        d_lo[at, lanes] = taken - high
        high, low = d_hi[...].astype(BF16), d_lo[...].astype(BF16)
        lowered = jnp.dot(high, w_hi[...], preferred_element_type=F32)
        lowered = lowered + jnp.dot(high, w_lo[...], preferred_element_type=F32)
        lowered = lowered + jnp.dot(low, w_hi[...], preferred_element_type=F32)
        for fr in (f0, f0 + 1):
            for row in range(4):
                for part in range(4):
                    at = (fr - f0) * 96 + row * 24 + part * 5
                    z_ref[fr, part * 20 + row * 5 : part * 20 + row * 5 + 5, :] = lowered[at : at + 5]
            lowered_ready(fr)

    def finish():
        for copy, cond in sent:
            when(cond, copy.wait_send)

    return finish


def dot_f32(a, b, dims=((1,), (0,))):
    return lax.dot_general(a, b, (dims, ((), ())), precision=highest, preferred_element_type=F32)


def attend_part(
    gain_ref, loads, wq_ref, wk_ref, wv_ref, wo_ref, z_ref, out_ref,
    keys, q_hi, q_lo, q_own, q_in, acc, best, total, part_acc, part_stat, result, landing, k_hi_ref, k_lo_ref,
    s1, r1, ss, rs, rets, retr,
):
    tile = lax.axis_index("tile")
    frame = lax.axis_index("frame")
    x, y, z = tile // 16, (tile // 4) % 4, tile % 4
    half, s = z // 2, z % 2
    zh, core = frame // 2, frame % 2

    def dev(x, y, z, core):
        return {"tile": x * 16 + y * 4 + z, "frame": zh * 2 + core}

    up = dev(x, (y + 1) % 4, z, core)
    down = dev(x, (y + 3) % 4, z, core)
    mate = dev(x, y, z + 1 - 2 * s, core)
    sibling = dev(x, y, z, 1 - core)
    sz = 2 * core + s
    crossed = half != core
    uncrossed = jnp.logical_not(crossed)

    from_z, from_core = 2 * core + y % 2, y // 2

    def greet(hello):
        for device in (up, down, mate, sibling):
            hello(device)
        for dx in range(1, 4):
            hello(dev((x + dx) % 4, y, sz, half))
        hello(dev(x, y, sz, half), crossed)
        expected = 7 + crossed.astype(jnp.int32)
        for j in range(4):
            hello(
                dev(x, j, from_z, from_core),
                jnp.logical_not((j == y) & (from_z == z) & (from_core == core)),
            )
            expected = expected + jnp.logical_not((sz == y) & (z == j) & (half == core)).astype(jnp.int32)
        return expected

    slot = s * 4 + y

    def block(b):
        return pl.ds(b * 80, 80)

    mine = pl.ds(pl.multiple_of(x * 80, 80), 80)

    def to_group(fr):
        return pltpu.make_async_remote_copy(
            src_ref=z_ref.at[fr],
            dst_ref=keys.at[slot, mine],
            send_sem=s1.at[fr],
            recv_sem=r1.at[x],
            device_id=dev(fr, y, sz, half),
            device_id_type=MESH,
        )

    def lowered_ready(fr):
        stays = uncrossed & (x == fr)

        @pl.when(jnp.logical_not(stays))
        def _():
            to_group(fr).start()

        @pl.when(stays)
        def _():
            keys[slot, mine, :] = z_ref[fr]

    def run():
        sent = []
        slot_up = s * 4 + (y + 1) % 4
        slot_down = s * 4 + (y + 3) % 4
        slot_far = s * 4 + (y + 2) % 4
        other = (1 - s) * 4
        mate_own, mate_up = other + y, other + (y + 1) % 4
        mate_down, mate_far = other + (y + 3) % 4, other + (y + 2) % 4

        def remote(src, dst, device, i):
            return pltpu.make_async_remote_copy(
                src_ref=src, dst_ref=dst, send_sem=ss.at[i], recv_sem=rs.at[i],
                device_id=device, device_id_type=MESH,
            )

        own_up, own_down, own_mate, mate_goes_up, mate_goes_down, far_on, far_mate = range(7)

        def push(kind, b, source, device):
            ref = keys.at[source, block(b)]
            copy = remote(ref, ref, device, kind * 4 + b)
            copy.start()
            sent.append(copy)

        def landed(kind, b, source):
            ref = keys.at[source, block(b)]
            remote(ref, ref, sibling, kind * 4 + b).wait_recv()

        for b in range(4):
            @pl.when(jnp.logical_not(uncrossed & (x == b)))
            def _():
                pltpu.make_async_remote_copy(
                    src_ref=z_ref.at[0],
                    dst_ref=keys.at[slot, block(b)],
                    send_sem=s1.at[b],
                    recv_sem=r1.at[b],
                    device_id=sibling,
                    device_id_type=MESH,
                ).wait_recv()

            push(own_up, b, slot, up)
            push(own_down, b, slot, down)
            push(own_mate, b, slot, mate)
        for load in loads:
            load.wait()

        gain = gain_ref[...]
        projected = dot_f32(norm(keys[slot], gain), wq_ref[...]) * (256.0 ** -0.5)
        q_own[...] = dot_f32(projected, wk_ref[...], ((1,), (1,)))
        q_copy = remote(q_own, q_in, sibling, 28)
        q_copy.start()
        sent.append(q_copy)
        q_hi[0:320], q_lo[0:320] = split(q_own[...])

        best[...] = jnp.full_like(best, -jnp.inf)
        total[...] = jnp.zeros_like(total)
        acc[...] = jnp.zeros_like(acc)

        def product(a, b, dims):
            return lax.dot_general(a, b, (dims, ((), ())), preferred_element_type=F32)

        def prepare(at, source):
            place = slice(at * 320, at * 320 + 320)
            k_hi_ref[place], k_lo_ref[place] = split(norm(keys[source], gain))

        def attend(start, stop, rows):
            k_hi, k_lo = k_hi_ref[start * 320 : stop * 320], k_lo_ref[start * 320 : stop * 320]
            across = ((1,), (1,))
            scores = product(q_hi[rows], k_hi, across) + product(q_hi[rows], k_lo, across)
            scores = scores + product(q_lo[rows], k_hi, across)
            old = best[rows]
            new = jnp.maximum(old, jnp.max(scores, axis=1, keepdims=True))
            factor = jnp.exp(old - new)
            weights = jnp.exp(scores - new)
            total[rows] = total[rows] * factor + jnp.sum(weights, axis=1, keepdims=True)
            best[rows] = new
            p_hi, p_lo = split(weights)
            along = ((1,), (0,))
            mixed = product(p_hi, k_hi, along) + product(p_hi, k_lo, along) + product(p_lo, k_hi, along)
            acc[rows] = acc[rows] * factor + mixed

        first, second, both = slice(0, 320), slice(320, 640), slice(0, 640)

        def forward(b):
            if b < 2:
                landed(own_up, b, slot_down)
                push(far_on, b, slot_down, up)
                landed(own_down, b, slot_up)
            else:
                landed(own_down, b, slot_up)
                push(far_on, b, slot_up, down)
                landed(own_up, b, slot_down)
            landed(own_mate, b, mate_own)
            push(mate_goes_up, b, mate_own, up)
            push(mate_goes_down, b, mate_own, down)

        def far_forward(b):
            landed(far_on, b, slot_far)
            push(far_mate, b, slot_far, mate)

        forward(0)
        prepare(0, slot)
        attend(0, 1, first)
        forward(1)
        q_copy.wait_recv()
        q_hi[320:640], q_lo[320:640] = split(q_in[...])
        attend(0, 1, second)
        forward(2)
        forward(3)
        prepare(1, slot_down)
        far_forward(0)
        prepare(2, slot_up)
        far_forward(1)
        far_forward(2)
        prepare(3, mate_own)
        far_forward(3)
        prepare(4, slot_far)
        attend(1, 5, both)
        for b in range(4):
            landed(mate_goes_up, b, mate_down)
        prepare(5, mate_down)
        for b in range(4):
            landed(mate_goes_down, b, mate_up)
        prepare(6, mate_up)
        for b in range(4):
            landed(far_mate, b, mate_far)
        prepare(7, mate_far)
        attend(5, 8, second)
        part_stat[0, :, 0:64] = jnp.broadcast_to(best[second], (320, 64))
        part_stat[0, :, 64:128] = jnp.broadcast_to(total[second], (320, 64))
        merge = [
            remote(part_stat.at[0], part_stat.at[1], sibling, 30),
            remote(acc.at[pl.ds(320, 320)], part_acc, sibling, 29),
        ]
        for copy in merge:
            copy.start()
        attend(5, 8, first)
        for copy in merge:
            copy.wait_recv()
        sent.extend(merge)
        other_best = part_stat[1, :, 0:1]
        other_total = part_stat[1, :, 64:65]
        top = jnp.maximum(best[first], other_best)
        mine_f = jnp.exp(best[first] - top)
        other_f = jnp.exp(other_best - top)
        whole = total[first] * mine_f + other_total * other_f
        mixed = (acc[first] * mine_f + part_acc[...] * other_f) / whole
        value = dot_f32(mixed, wv_ref[...])
        y_out = keys[slot] + dot_f32(value, wo_ref[...])

        backs = []
        for part in range(4):
            for b in range(4):
                start = b * 80 + part * 20
                result[part, b] = y_out[start : start + 20]
            copy = pltpu.make_async_remote_copy(
                src_ref=result.at[part],
                dst_ref=landing.at[:, y],
                send_sem=rets.at[part],
                recv_sem=retr.at[y],
                device_id=dev(x, sz, part, half),
                device_id_type=MESH,
            )
            stays = (sz == y) & (z == part) & (half == core)
            backs.append((copy, stays))

            @pl.when(jnp.logical_not(stays))
            def _():
                copy.start()

            @pl.when(stays)
            def _():
                landing[:, pl.ds(y, 1), :, :] = result[part][:, None]

        for sy in range(4):
            here = (sy == y) & (from_z == z) & (from_core == core)

            @pl.when(jnp.logical_not(here))
            def _():
                pltpu.make_async_remote_copy(
                    src_ref=result.at[0],
                    dst_ref=landing.at[:, sy],
                    send_sem=rets.at[0],
                    recv_sem=retr.at[sy],
                    device_id=sibling,
                    device_id_type=MESH,
                ).wait_recv()

            for sx in range(4):
                at = (sx * 4 + sy) * 20
                out_ref[0, at : at + 20, :] = landing[sx, sy]

        for fr in range(4):
            @pl.when(jnp.logical_not(uncrossed & (x == fr)))
            def _():
                to_group(fr).wait_send()

        for copy in sent:
            copy.wait_send()
        for copy, stays in backs:
            @pl.when(jnp.logical_not(stays))
            def _():
                copy.wait_send()

    return greet, lowered_ready, run


CONV_SCRATCH = [
    ((4, 2, 160, 128), F32), ((2, 1152, 128), F32), ((2, 384, 128), F32), ((1152, 256), F32),
    ((4, 8, 40, 128), F32), ((3, 4, 10, 56, 128), F32), ((4, 4, 4, 1, 128), F32), ((4, 4, 4, 1, 128), F32),
    ((2, 2, 4, 8, 1, 128), F32), ((2, 2, 4, 8, 1, 128), F32), ((2, 4, 4, 1, 128), F32), ((2, 4, 4, 1, 128), F32),
    ((2, 2, 320, 128), F32), ((2, 2, 320, 128), F32), ((320, 768), BF16), ((320, 768), BF16),
    ((2, 320, 1152), BF16), ((2, 320, 1152), BF16), ((192, 1152), F32), ((192, 1152), F32),
    ((2, 1152, 256), BF16), ((2, 384, 256), BF16), ((1152, 256), BF16), ((1152, 256), BF16),
]
ATTEND_SCRATCH = [
    ((8, 320, 256), F32), ((640, 256), BF16), ((640, 256), BF16), ((320, 256), F32), ((320, 256), F32),
    ((640, 256), F32), ((640, 1), F32), ((640, 1), F32), ((320, 256), F32), ((2, 320, 128), F32),
    ((4, 4, 20, 256), F32), ((4, 4, 20, 256), F32), ((2560, 256), BF16), ((2560, 256), BF16),
]
CONV_SEMS = (56, 56)
ATTEND_SEMS = (4, 4, 31, 31, 4, 4)


def encode_kernel(
    video_hbm, space_hbm, time_hbm, down_hbm, wq_hbm, wk_hbm, wv_hbm, wo_hbm, gain_ref, attn_gain_ref, out_ref,
    z_ref, wq_ref, wk_ref, wv_ref, wo_ref, load_sems, *scratch,
):
    c, a = len(CONV_SCRATCH), len(ATTEND_SCRATCH)
    conv_scratch, attend_scratch = scratch[:c], scratch[c : c + a]
    conv_sems, attend_sems = scratch[c + a : c + a + 2], scratch[c + a + 2 :]
    pairs = ((wq_hbm, wq_ref), (wk_hbm, wk_ref), (wv_hbm, wv_ref), (wo_hbm, wo_ref))
    loads = [pltpu.make_async_copy(src, dst, load_sems.at[4 + i]) for i, (src, dst) in enumerate(pairs)]
    greet, lowered_ready, attend = attend_part(
        attn_gain_ref, loads, wq_ref, wk_ref, wv_ref, wo_ref, z_ref, out_ref, *attend_scratch, *attend_sems
    )
    for load in loads:
        load.start()
    finish = conv_part(
        video_hbm, space_hbm, time_hbm, down_hbm, gain_ref, z_ref, *conv_scratch, *conv_sems,
        load_sems, greet, lowered_ready,
    )
    attend()
    finish()


def local(
    video,
    norm_gain,
    space_weight,
    time_weight,
    down_weight,
    attn_gain,
    w_query,
    w_key,
    w_value,
    w_out,
):
    vmem = pl.BlockSpec(memory_space=pltpu.VMEM)
    hbm = pl.BlockSpec(memory_space=pltpu.HBM)
    dma = pltpu.SemaphoreType.DMA
    square = pltpu.VMEM((256, 256), F32)
    return pl.pallas_call(
        encode_kernel,
        out_shape=jax.ShapeDtypeStruct((1, 320, 256), F32),
        in_specs=[hbm] * 8 + [vmem] * 2,
        out_specs=vmem,
        scratch_shapes=[
            pltpu.VMEM((4, 80, 256), F32), square, square, square, square, dma((8,)),
            *[pltpu.VMEM(shape, dtype) for shape, dtype in CONV_SCRATCH + ATTEND_SCRATCH],
            *[dma((count,)) for count in CONV_SEMS + ATTEND_SEMS],
        ],
        compiler_params=pltpu.CompilerParams(
            collective_id=3, has_side_effects=True, vmem_limit_bytes=56 * 2**20
        ),
        name="encode",
    )(
        video, space_weight.reshape(2, 1152, 128), time_weight.reshape(2, 384, 128), down_weight.reshape(1152, 256),
        w_query, w_key, w_value, w_out, norm_gain, attn_gain.reshape(1, 256),
    )


def solution(mesh):
    in_specs = (P("frame", "tile", None, None), P(), P(), P(), P(), P(), P(), P(), P(), P())
    out_specs = P(("frame", "tile"), None, None)
    return jax.shard_map(local, mesh=mesh, in_specs=in_specs, out_specs=out_specs, check_vma=False)
```

time: 107 us -> 105 us (0.981)
  local copies, waits for them, and re-layouts: 6.08 us -> 1.72 us
  Pallas kernels: 101 us -> 103 us
    unnamed x20 -> x1, local copies, waits for them, and re-layouts: 5.32 us -> 1.72 us
    pallas_call x2 -> x1, Pallas kernels: 101 us -> 103 us  [local(): pl.pallas_call(encode_kernel, out_shape=jax.ShapeDtypeStruct((1, 320, 256...]
where the time goes in v2:
time: 105 us
  Pallas kernels  103 us (98%)
  local copies, waits for them, and re-layouts  1.72 us (2%)
    pallas_call x1, Pallas kernels, local(): pl.pallas_call(encode_kernel, out_shape=jax.ShapeDtypeStruct((1, 320, 256...  103 us

profile of v2, /device:TPU:232, one launch (start us, length us, event | category | flops | bytes accessed | tf_op | source)
XLA Modules:
  0.0 104.8 jit_solution(287700766043261120)
XLA Ops:
  0.0 103.0 %encode.1 = f32[1,320,256]{2,1,0:T(8,128)} custom-call(f32[4,2,160,128]{3,2,1,0:T(8,128)} %video_hbm.1, f32[2,1152,128]{2,1,0:T(8,128)} %bitcast.4, f32[2,384,128]{2,1,0:T(8,128)} %bitcast.6, f32[1152,256]{1,0:T(8,128)} %bitcast.5, f32[256,256]{1,0:T(8,128)} %wq_hbm.1, f32[256,256]{1,0:T(8,128)} %wk_hbm.1, f32[256,256]{1,0:T(8,128)} %wv_hbm.1, ...), custom_call_target="tpu_custom_call" | custom-call | tf_op jit(solution)/shard_map/encode/pallas_call | solution.py:683
  103.0 1.7 %copy.12 = f32[1,320,256]{2,1,0:T(8,128)} copy(f32[1,320,256]{2,1,0:T(8,128)} %encode.1) | data formatting | bytes 655360

commit v3 on v2

--- a/solution.py
+++ b/solution.py
@@ -33,7 +33,7 @@
     video_ref, space_ref, time_ref, down_ref,
     state, padded, ext, ext_in, cols, cols_in, corners, corners_in,
     late, late_in, u_hi, u_lo, a_hi, a_lo, d_hi, d_lo, w_space, w_time, w_hi, w_lo,
-    send_sems, recv_sems, load_sems, greet, lowered_ready,
+    send_sems, recv_sems, load_sems, greet, weights_ready, lowered_ready,
 ):
     tile = lax.axis_index("tile")
     frame = lax.axis_index("frame")
@@ -152,6 +152,7 @@
         high, low = split(down_ref[rows, :])
         w_hi[rows, :] = high
         w_lo[rows, :] = low
+    weights_ready()
 
     def two_part(high, low, weight):
         both = jnp.dot(high, weight, preferred_element_type=F32)
@@ -269,7 +270,7 @@
     for dz in range(1, 4):
         arrived(("ext", dz), ext_in.at[(z + dz) % 4])
     gain = gain_ref[0, 0:1, :]
-    for at, fr in enumerate(order):
+    for fr in order:
         for dz in range(1, 4):
             arrived(("band", fr, dz), state.at[fr, pl.ds(((z + dz) % 4) * 2, 2)])
         padded[0, fr, 1:9, 8:48, :] = act(state[fr].reshape(320, 128), gain).reshape(8, 40, 128)
@@ -285,11 +286,9 @@
             def _():
                 padded[0, fr, rows, RIGHT : RIGHT + 1, :] = fringe[2:4]
         send_rows(0, fr, 1, slice(None))
-        if at > 0:
-            rows_arrived(0, order[at - 1], 1, slice(None))
-            conv(0, order[at - 1])
-    rows_arrived(0, order[3], 1, slice(None))
-    conv(0, order[3])
+    for fr in order:
+        rows_arrived(0, fr, 1, slice(None))
+        conv(0, fr)
 
     gain = gain_ref[1, 0:1, :]
 
@@ -302,14 +301,12 @@
         send_edges(1, f0, 2)
 
     middle(2)
-    edges_arrived(1, 2, 2)
-    for fr in (2, 3):
-        conv(1, fr)
     earlier(0)
     middle(0)
-    edges_arrived(1, 0, 2)
-    for fr in (0, 1):
-        conv(1, fr)
+    for f0 in (2, 0):
+        edges_arrived(1, f0, 2)
+        for fr in (f0, f0 + 1):
+            conv(1, fr)
     for f0 in (2, 0):
         if f0 == 0:
             earlier(1)
@@ -318,18 +315,24 @@
         send_rows(2, f0, 2, inner, False)
         send_edges(2, f0, 2, False)
 
+    def take(f0, row, dy, dx):
+        lanes = slice((dy * 3 + dx) * 128, (dy * 3 + dx) * 128 + 128)
+        for fr in (f0, f0 + 1):
+            at = slice((fr - f0) * 96 + row * 24, (fr - f0) * 96 + row * 24 + 24)
+            taken = padded[2, fr, 2 * row + dy, pl.ds(LEFT + dx, 24, stride=2), :]
+            high = taken.astype(BF16).astype(F32)
+            d_hi[at, lanes] = high
+            d_lo[at, lanes] = taken - high
+
+    taps = [(row, dy, dx) for row in range(4) for dy in range(3) for dx in range(3)]
     for f0 in (2, 0):
+        for row, dy, dx in taps:
+            if dx > 0 and row + dy > 0:
+                take(f0, row, dy, dx)
         edges_arrived(2, f0, 2, False)
-        for fr in (f0, f0 + 1):
-            for row in range(4):
-                at = slice((fr - f0) * 96 + row * 24, (fr - f0) * 96 + row * 24 + 24)
-                for dy in range(3):
-                    for dx in range(3):
-                        taken = padded[2, fr, 2 * row + dy, pl.ds(LEFT + dx, 24, stride=2), :]
-                        lanes = slice((dy * 3 + dx) * 128, (dy * 3 + dx) * 128 + 128)
-                        high = taken.astype(BF16).astype(F32)
-                        d_hi[at, lanes] = high
-                        d_lo[at, lanes] = taken - high
+        for row, dy, dx in taps:
+            if dx == 0 or row + dy == 0:
+                take(f0, row, dy, dx)
         high, low = d_hi[...].astype(BF16), d_lo[...].astype(BF16)
         lowered = jnp.dot(high, w_hi[...], preferred_element_type=F32)
         lowered = lowered + jnp.dot(high, w_lo[...], preferred_element_type=F32)
@@ -354,7 +357,7 @@
 
 def attend_part(
     gain_ref, loads, wq_ref, wk_ref, wv_ref, wo_ref, z_ref, out_ref,
-    keys, q_hi, q_lo, q_own, q_in, acc, best, total, part_acc, part_stat, result, landing, k_hi_ref, k_lo_ref,
+    keys, q_ref, q_own, q_in, acc, best, total, part_acc, part_stat, result, landing, k_ref, own_z, w_qk, w_vo,
     s1, r1, ss, rs, rets, retr,
 ):
     tile = lax.axis_index("tile")
@@ -401,7 +404,7 @@
     def to_group(fr):
         return pltpu.make_async_remote_copy(
             src_ref=z_ref.at[fr],
-            dst_ref=keys.at[slot, mine],
+            dst_ref=own_z.at[mine],
             send_sem=s1.at[fr],
             recv_sem=r1.at[x],
             device_id=dev(fr, y, sz, half),
@@ -417,7 +420,20 @@
 
         @pl.when(stays)
         def _():
-            keys[slot, mine, :] = z_ref[fr]
+            own_z[mine, :] = z_ref[fr]
+
+    def weights_ready():
+        for load in loads:
+            load.wait()
+        together = dot_f32(wq_ref[...], wk_ref[...], ((1,), (1,))) * (256.0 ** -0.5 * 1.4426950408889634)
+        w_qk[0], w_qk[1] = split(together)
+        w_vo[0], w_vo[1] = split(dot_f32(wv_ref[...], wo_ref[...]))
+
+    def three_part(values, weight):
+        high, low = split(values)
+        total = jnp.dot(high, weight[0], preferred_element_type=F32)
+        total = total + jnp.dot(high, weight[1], preferred_element_type=F32)
+        return total + jnp.dot(low, weight[0], preferred_element_type=F32)
 
     def run():
         sent = []
@@ -446,31 +462,35 @@
             ref = keys.at[source, block(b)]
             remote(ref, ref, sibling, kind * 4 + b).wait_recv()
 
+        gain = gain_ref[...]
         for b in range(4):
             @pl.when(jnp.logical_not(uncrossed & (x == b)))
             def _():
                 pltpu.make_async_remote_copy(
                     src_ref=z_ref.at[0],
-                    dst_ref=keys.at[slot, block(b)],
+                    dst_ref=own_z.at[block(b)],
                     send_sem=s1.at[b],
                     recv_sem=r1.at[b],
                     device_id=sibling,
                     device_id_type=MESH,
                 ).wait_recv()
 
+            keys[slot, block(b), :] = norm(own_z[block(b)], gain)
             push(own_up, b, slot, up)
             push(own_down, b, slot, down)
             push(own_mate, b, slot, mate)
-        for load in loads:
-            load.wait()
-
-        gain = gain_ref[...]
-        projected = dot_f32(norm(keys[slot], gain), wq_ref[...]) * (256.0 ** -0.5)
-        q_own[...] = dot_f32(projected, wk_ref[...], ((1,), (1,)))
+        def place_query(at, values):
+            rows = slice(at, at + 320)
+            high, low = split(values[...])
+            q_ref[rows, 0:256] = high
+            q_ref[rows, 256:512] = low
+            q_ref[rows, 512:768] = high
+
+        q_own[...] = three_part(keys[slot], w_qk)
         q_copy = remote(q_own, q_in, sibling, 28)
         q_copy.start()
         sent.append(q_copy)
-        q_hi[0:320], q_lo[0:320] = split(q_own[...])
+        place_query(0, q_own)
 
         best[...] = jnp.full_like(best, -jnp.inf)
         total[...] = jnp.zeros_like(total)
@@ -481,17 +501,19 @@
 
         def prepare(at, source):
             place = slice(at * 320, at * 320 + 320)
-            k_hi_ref[place], k_lo_ref[place] = split(norm(keys[source], gain))
+            high, low = split(keys[source])
+            k_ref[place, 0:256] = high
+            k_ref[place, 256:512] = high
+            k_ref[place, 512:768] = low
 
         def attend(start, stop, rows):
-            k_hi, k_lo = k_hi_ref[start * 320 : stop * 320], k_lo_ref[start * 320 : stop * 320]
-            across = ((1,), (1,))
-            scores = product(q_hi[rows], k_hi, across) + product(q_hi[rows], k_lo, across)
-            scores = scores + product(q_lo[rows], k_hi, across)
+            place = slice(start * 320, stop * 320)
+            k_hi, k_lo = k_ref[place, 0:256], k_ref[place, 512:768]
+            scores = product(q_ref[rows], k_ref[place], ((1,), (1,)))
             old = best[rows]
             new = jnp.maximum(old, jnp.max(scores, axis=1, keepdims=True))
-            factor = jnp.exp(old - new)
-            weights = jnp.exp(scores - new)
+            factor = jnp.exp2(old - new)
+            weights = jnp.exp2(scores - new)
             total[rows] = total[rows] * factor + jnp.sum(weights, axis=1, keepdims=True)
             best[rows] = new
             p_hi, p_lo = split(weights)
@@ -499,7 +521,7 @@
             mixed = product(p_hi, k_hi, along) + product(p_hi, k_lo, along) + product(p_lo, k_hi, along)
             acc[rows] = acc[rows] * factor + mixed
 
-        first, second, both = slice(0, 320), slice(320, 640), slice(0, 640)
+        first, second = slice(0, 320), slice(320, 640)
 
         def forward(b):
             if b < 2:
@@ -523,7 +545,7 @@
         attend(0, 1, first)
         forward(1)
         q_copy.wait_recv()
-        q_hi[320:640], q_lo[320:640] = split(q_in[...])
+        place_query(320, q_in)
         attend(0, 1, second)
         forward(2)
         forward(3)
@@ -535,7 +557,8 @@
         prepare(3, mate_own)
         far_forward(3)
         prepare(4, slot_far)
-        attend(1, 5, both)
+        attend(1, 5, second)
+        attend(1, 5, first)
         for b in range(4):
             landed(mate_goes_up, b, mate_down)
         prepare(5, mate_down)
@@ -561,21 +584,20 @@
         other_best = part_stat[1, :, 0:1]
         other_total = part_stat[1, :, 64:65]
         top = jnp.maximum(best[first], other_best)
-        mine_f = jnp.exp(best[first] - top)
-        other_f = jnp.exp(other_best - top)
+        mine_f = jnp.exp2(best[first] - top)
+        other_f = jnp.exp2(other_best - top)
         whole = total[first] * mine_f + other_total * other_f
         mixed = (acc[first] * mine_f + part_acc[...] * other_f) / whole
-        value = dot_f32(mixed, wv_ref[...])
-        y_out = keys[slot] + dot_f32(value, wo_ref[...])
+        y_out = own_z[...] + three_part(mixed, w_vo)
 
         backs = []
         for part in range(4):
             for b in range(4):
                 start = b * 80 + part * 20
-                result[part, b] = y_out[start : start + 20]
+                result[part, b * 20 : b * 20 + 20] = y_out[start : start + 20]
             copy = pltpu.make_async_remote_copy(
                 src_ref=result.at[part],
-                dst_ref=landing.at[:, y],
+                dst_ref=landing.at[y],
                 send_sem=rets.at[part],
                 recv_sem=retr.at[y],
                 device_id=dev(x, sz, part, half),
@@ -590,7 +612,7 @@
 
             @pl.when(stays)
             def _():
-                landing[:, pl.ds(y, 1), :, :] = result[part][:, None]
+                landing[y] = result[part]
 
         for sy in range(4):
             here = (sy == y) & (from_z == z) & (from_core == core)
@@ -599,7 +621,7 @@
             def _():
                 pltpu.make_async_remote_copy(
                     src_ref=result.at[0],
-                    dst_ref=landing.at[:, sy],
+                    dst_ref=landing.at[sy],
                     send_sem=rets.at[0],
                     recv_sem=retr.at[sy],
                     device_id=sibling,
@@ -608,7 +630,7 @@
 
             for sx in range(4):
                 at = (sx * 4 + sy) * 20
-                out_ref[0, at : at + 20, :] = landing[sx, sy]
+                out_ref[0, at : at + 20, :] = landing[sy, sx * 20 : sx * 20 + 20]
 
         for fr in range(4):
             @pl.when(jnp.logical_not(uncrossed & (x == fr)))
@@ -622,7 +644,7 @@
             def _():
                 copy.wait_send()
 
-    return greet, lowered_ready, run
+    return greet, weights_ready, lowered_ready, run
 
 
 CONV_SCRATCH = [
@@ -634,9 +656,10 @@
     ((2, 1152, 256), BF16), ((2, 384, 256), BF16), ((1152, 256), BF16), ((1152, 256), BF16),
 ]
 ATTEND_SCRATCH = [
-    ((8, 320, 256), F32), ((640, 256), BF16), ((640, 256), BF16), ((320, 256), F32), ((320, 256), F32),
+    ((8, 320, 256), F32), ((640, 768), BF16), ((320, 256), F32), ((320, 256), F32),
     ((640, 256), F32), ((640, 1), F32), ((640, 1), F32), ((320, 256), F32), ((2, 320, 128), F32),
-    ((4, 4, 20, 256), F32), ((4, 4, 20, 256), F32), ((2560, 256), BF16), ((2560, 256), BF16),
+    ((4, 80, 256), F32), ((4, 80, 256), F32), ((2560, 768), BF16),
+    ((320, 256), F32), ((2, 256, 256), BF16), ((2, 256, 256), BF16),
 ]
 CONV_SEMS = (56, 56)
 ATTEND_SEMS = (4, 4, 31, 31, 4, 4)
@@ -651,14 +674,14 @@
     conv_sems, attend_sems = scratch[c + a : c + a + 2], scratch[c + a + 2 :]
     pairs = ((wq_hbm, wq_ref), (wk_hbm, wk_ref), (wv_hbm, wv_ref), (wo_hbm, wo_ref))
     loads = [pltpu.make_async_copy(src, dst, load_sems.at[4 + i]) for i, (src, dst) in enumerate(pairs)]
-    greet, lowered_ready, attend = attend_part(
+    greet, weights_ready, lowered_ready, attend = attend_part(
         attn_gain_ref, loads, wq_ref, wk_ref, wv_ref, wo_ref, z_ref, out_ref, *attend_scratch, *attend_sems
     )
     for load in loads:
         load.start()
     finish = conv_part(
         video_hbm, space_hbm, time_hbm, down_hbm, gain_ref, z_ref, *conv_scratch, *conv_sems,
-        load_sems, greet, lowered_ready,
+        load_sems, greet, weights_ready, lowered_ready,
     )
     attend()
     finish()

time: 105 us -> 97.3 us (0.927)
  Pallas kernels: 103 us -> 95.4 us
    pallas_call x1, Pallas kernels: 103 us -> 95.4 us  [local(): pl.pallas_call(encode_kernel, out_shape=jax.ShapeDtypeStruct((1, 320, 256...]
where the time goes in v3:
time: 97.3 us; the launch traced here: 97.1 us
  Pallas kernels  95.4 us (98%)
  local copies, waits for them, and re-layouts  1.72 us (2%)
    pallas_call x1, Pallas kernels, local(): pl.pallas_call(encode_kernel, out_shape=jax.ShapeDtypeStruct((1, 320, 256...  95.4 us

profile of v3, /device:TPU:232, one launch (start us, length us, event | category | flops | bytes accessed | tf_op | source)
XLA Modules:
  0.0 97.1 jit_solution(5006284610507279477)
XLA Ops:
  0.0 95.4 %encode.1 = f32[1,320,256]{2,1,0:T(8,128)} custom-call(f32[4,2,160,128]{3,2,1,0:T(8,128)} %video_hbm.1, f32[2,1152,128]{2,1,0:T(8,128)} %bitcast.4, f32[2,384,128]{2,1,0:T(8,128)} %bitcast.6, f32[1152,256]{1,0:T(8,128)} %bitcast.5, f32[256,256]{1,0:T(8,128)} %wq_hbm.1, f32[256,256]{1,0:T(8,128)} %wk_hbm.1, f32[256,256]{1,0:T(8,128)} %wv_hbm.1, ...), custom_call_target="tpu_custom_call" | custom-call | tf_op jit(solution)/shard_map/encode/pallas_call | solution.py:706
  95.4 1.7 %copy.12 = f32[1,320,256]{2,1,0:T(8,128)} copy(f32[1,320,256]{2,1,0:T(8,128)} %encode.1) | data formatting | bytes 655360

commit v4 on v3

--- a/solution.py
+++ b/solution.py
@@ -113,10 +113,18 @@
     def band(part):
         return pl.ds(pl.multiple_of(part * 40, 8), 40)
 
-    for fr in order:
+    def send_bands(fr):
         for dz in (2, 1, 3):
             part = (z + dz) % 4
             start(("band", fr, dz), video_hbm.at[fr, :, band(part), :], state.at[fr, pl.ds(z * 2, 2)], dev(k, part))
+
+    def bands_left():
+        for copy, _ in sent[:3]:
+            copy.wait_send()
+        sent[:3] = []
+
+    send_bands(2)
+    send_bands(3)
     loads[0].wait()
     for part in range(4):
         for fr in range(4):
@@ -267,10 +275,16 @@
         lanes = slice(fr * 128, fr * 128 + 384)
         return state[fr].reshape(320, 128) + two_part(u_hi[:, lanes], u_lo[:, lanes], w_time[b])
 
+    bands_left()
+    send_bands(0)
+
     for dz in range(1, 4):
         arrived(("ext", dz), ext_in.at[(z + dz) % 4])
     gain = gain_ref[0, 0:1, :]
     for fr in order:
+        if fr == 3:
+            bands_left()
+            send_bands(1)
         for dz in range(1, 4):
             arrived(("band", fr, dz), state.at[fr, pl.ds(((z + dz) % 4) * 2, 2)])
         padded[0, fr, 1:9, 8:48, :] = act(state[fr].reshape(320, 128), gain).reshape(8, 40, 128)
@@ -286,7 +300,10 @@
             def _():
                 padded[0, fr, rows, RIGHT : RIGHT + 1, :] = fringe[2:4]
         send_rows(0, fr, 1, slice(None))
-    for fr in order:
+        if fr < 2:
+            rows_arrived(0, fr + 2, 1, slice(None))
+            conv(0, fr + 2)
+    for fr in (0, 1):
         rows_arrived(0, fr, 1, slice(None))
         conv(0, fr)
 

time: 97.3 us -> 92.5 us (0.951)
  Pallas kernels: 95.4 us -> 90.4 us
    pallas_call x1, Pallas kernels: 95.4 us -> 90.4 us  [local(): pl.pallas_call(encode_kernel, out_shape=jax.ShapeDtypeStruct((1, 320, 256...]
where the time goes in v4:
time: 92.5 us; the launch traced here: 92.1 us
  Pallas kernels  90.4 us (98%)
  local copies, waits for them, and re-layouts  1.72 us (2%)
    pallas_call x1, Pallas kernels, local(): pl.pallas_call(encode_kernel, out_shape=jax.ShapeDtypeStruct((1, 320, 256...  90.4 us

profile of v4, /device:TPU:232, one launch (start us, length us, event | category | flops | bytes accessed | tf_op | source)
XLA Modules:
  0.0 92.1 jit_solution(14236820348516003840)
XLA Ops:
  0.0 90.4 %encode.1 = f32[1,320,256]{2,1,0:T(8,128)} custom-call(f32[4,2,160,128]{3,2,1,0:T(8,128)} %video_hbm.1, f32[2,1152,128]{2,1,0:T(8,128)} %bitcast.4, f32[2,384,128]{2,1,0:T(8,128)} %bitcast.6, f32[1152,256]{1,0:T(8,128)} %bitcast.5, f32[256,256]{1,0:T(8,128)} %wq_hbm.1, f32[256,256]{1,0:T(8,128)} %wk_hbm.1, f32[256,256]{1,0:T(8,128)} %wv_hbm.1, ...), custom_call_target="tpu_custom_call" | custom-call | tf_op jit(solution)/shard_map/encode/pallas_call | solution.py:723
  90.4 1.7 %copy.12 = f32[1,320,256]{2,1,0:T(8,128)} copy(f32[1,320,256]{2,1,0:T(8,128)} %encode.1) | data formatting | bytes 655360

commit v5 on v4

--- a/solution.py
+++ b/solution.py
@@ -114,17 +114,18 @@
         return pl.ds(pl.multiple_of(part * 40, 8), 40)
 
     def send_bands(fr):
-        for dz in (2, 1, 3):
+        for dz in (1, 3, 2):
             part = (z + dz) % 4
             start(("band", fr, dz), video_hbm.at[fr, :, band(part), :], state.at[fr, pl.ds(z * 2, 2)], dev(k, part))
-
-    def bands_left():
-        for copy, _ in sent[:3]:
+        bands = sent[-3:]
+        del sent[-3:]
+        return bands
+
+    def bands_left(bands):
+        for copy, _ in bands:
             copy.wait_send()
-        sent[:3] = []
-
-    send_bands(2)
-    send_bands(3)
+
+    bands = send_bands(2)
     loads[0].wait()
     for part in range(4):
         for fr in range(4):
@@ -143,6 +144,9 @@
     ext_in[z] = ext[z]
     for fr in range(4):
         state[fr, pl.ds(z * 2, 2)] = video_ref[fr, :, band(z), :]
+
+    bands_left(bands)
+    bands = send_bands(3)
 
     for load in loads[1:]:
         load.wait()
@@ -275,16 +279,15 @@
         lanes = slice(fr * 128, fr * 128 + 384)
         return state[fr].reshape(320, 128) + two_part(u_hi[:, lanes], u_lo[:, lanes], w_time[b])
 
-    bands_left()
-    send_bands(0)
+    bands_left(bands)
+    sent.extend(send_bands(0))
 
     for dz in range(1, 4):
         arrived(("ext", dz), ext_in.at[(z + dz) % 4])
     gain = gain_ref[0, 0:1, :]
     for fr in order:
         if fr == 3:
-            bands_left()
-            send_bands(1)
+            sent.extend(send_bands(1))
         for dz in range(1, 4):
             arrived(("band", fr, dz), state.at[fr, pl.ds(((z + dz) % 4) * 2, 2)])
         padded[0, fr, 1:9, 8:48, :] = act(state[fr].reshape(320, 128), gain).reshape(8, 40, 128)

time: 92.5 us -> 91.6 us (level)
  no operation moved by 1% of the time
where the time goes in v5:
time: 91.6 us; the launch traced here: 91.4 us
  Pallas kernels  89.7 us (98%)
  local copies, waits for them, and re-layouts  1.72 us (2%)
    pallas_call x1, Pallas kernels, local(): pl.pallas_call(encode_kernel, out_shape=jax.ShapeDtypeStruct((1, 320, 256...  89.7 us

profile of v5, /device:TPU:232, one launch (start us, length us, event | category | flops | bytes accessed | tf_op | source)
XLA Modules:
  0.0 91.4 jit_solution(17489933521536798653)
XLA Ops:
  0.0 89.7 %encode.1 = f32[1,320,256]{2,1,0:T(8,128)} custom-call(f32[4,2,160,128]{3,2,1,0:T(8,128)} %video_hbm.1, f32[2,1152,128]{2,1,0:T(8,128)} %bitcast.4, f32[2,384,128]{2,1,0:T(8,128)} %bitcast.6, f32[1152,256]{1,0:T(8,128)} %bitcast.5, f32[256,256]{1,0:T(8,128)} %wq_hbm.1, f32[256,256]{1,0:T(8,128)} %wk_hbm.1, f32[256,256]{1,0:T(8,128)} %wv_hbm.1, ...), custom_call_target="tpu_custom_call" | custom-call | tf_op jit(solution)/shard_map/encode/pallas_call | solution.py:726
  89.7 1.7 %copy.12 = f32[1,320,256]{2,1,0:T(8,128)} copy(f32[1,320,256]{2,1,0:T(8,128)} %encode.1) | data formatting | bytes 655360

commit v6 on v5

--- a/solution.py
+++ b/solution.py
@@ -280,13 +280,14 @@
         return state[fr].reshape(320, 128) + two_part(u_hi[:, lanes], u_lo[:, lanes], w_time[b])
 
     bands_left(bands)
-    sent.extend(send_bands(0))
+    bands = send_bands(0)
 
     for dz in range(1, 4):
         arrived(("ext", dz), ext_in.at[(z + dz) % 4])
     gain = gain_ref[0, 0:1, :]
     for fr in order:
-        if fr == 3:
+        if fr == 0:
+            bands_left(bands)
             sent.extend(send_bands(1))
         for dz in range(1, 4):
             arrived(("band", fr, dz), state.at[fr, pl.ds(((z + dz) % 4) * 2, 2)])

time: 91.6 us -> 92.9 us (1.014)
  Pallas kernels: 89.7 us -> 91.1 us
    pallas_call x1, Pallas kernels: 89.7 us -> 91.1 us  [local(): pl.pallas_call(encode_kernel, out_shape=jax.ShapeDtypeStruct((1, 320, 256...]
where the time goes in v6:
time: 92.9 us; the launch traced here: 92.8 us
  Pallas kernels  91.1 us (98%)
  local copies, waits for them, and re-layouts  1.72 us (2%)
    pallas_call x1, Pallas kernels, local(): pl.pallas_call(encode_kernel, out_shape=jax.ShapeDtypeStruct((1, 320, 256...  91.1 us

profile of v6, /device:TPU:232, one launch (start us, length us, event | category | flops | bytes accessed | tf_op | source)
XLA Modules:
  0.0 92.8 jit_solution(17756479788356089362)
XLA Ops:
  0.0 91.1 %encode.1 = f32[1,320,256]{2,1,0:T(8,128)} custom-call(f32[4,2,160,128]{3,2,1,0:T(8,128)} %video_hbm.1, f32[2,1152,128]{2,1,0:T(8,128)} %bitcast.4, f32[2,384,128]{2,1,0:T(8,128)} %bitcast.6, f32[1152,256]{1,0:T(8,128)} %bitcast.5, f32[256,256]{1,0:T(8,128)} %wq_hbm.1, f32[256,256]{1,0:T(8,128)} %wk_hbm.1, f32[256,256]{1,0:T(8,128)} %wv_hbm.1, ...), custom_call_target="tpu_custom_call" | custom-call | tf_op jit(solution)/shard_map/encode/pallas_call | solution.py:727
  91.1 1.7 %copy.12 = f32[1,320,256]{2,1,0:T(8,128)} copy(f32[1,320,256]{2,1,0:T(8,128)} %encode.1) | data formatting | bytes 655360
